TPU v7x, 512 devices: a whole 4x8x8 slice. The times are simulated.
512 devices in a mesh: leaf: 128 (over z, y, core), rhs: 4 (over x).
Axes of the slice: x: 4, y: 8, z: 8, core: 2. Of those that a mesh axis runs over, the one named last changes fastest.
Arguments:
- right_side: bfloat16 [64, 524288], P(None, ('leaf', 'rhs')), may hold values from -6 to 6
- point_order: int32 [524288], P('leaf'), may hold values from 0 to 4095, as said below
- leaf_inverse: bfloat16 [1024, 512, 512], P('leaf', 'rhs')
- leaf_basis: bfloat16 [1024, 512, 256], P('leaf', 'rhs'), may hold values from -0.25 to 0.25
- leaf_coupling: bfloat16 [1024, 512, 256], P('leaf', 'rhs'), may hold values from -0.1875 to 0.1875
- node_inverse: bfloat16 [1024, 512, 512], P('leaf', 'rhs')
- node_basis: bfloat16 [1024, 512, 256], P('leaf', 'rhs'), may hold values from -0.25 to 0.25
- node_coupling: bfloat16 [1024, 512, 256], P('leaf', 'rhs'), may hold values from -0.375 to 0.375
Outputs:
- coefficients: float32 [1024, 64, 512], P('leaf', None, 'rhs')
Inputs may be any that keep to these rules, and one draw needn't show every extreme that they name: `point_order`: within each block of 4096 entries that one index of leaf holds, every number from 0 to 4095 stands once.
All inputs are finite; a program needn't handle non-finite values.
Results may differ from a plain program's by a relative error of at most 0.03.
Values may be sent and summed in bfloat16 or wider, within the bound.
A program may use at most 64 MiB of HBM per device.

v0:
```python
import jax
import jax.numpy as jnp
from jax import lax
from jax.sharding import PartitionSpec as P


def from_behind(block, axis, distance):
    devices = range(lax.axis_size(axis))
    route = [(i - distance, i) for i in devices if i - distance in devices]
    return lax.ppermute(block, axis, route)


def fetch_child(values, offset_by):
    return from_behind(values, "leaf", offset_by)


def send_share(values, offset_by):
    return from_behind(values, "leaf", offset_by)


def body(
    right_side,
    point_order,
    leaf_inverse,
    leaf_basis,
    leaf_coupling,
    node_inverse,
    node_basis,
    node_coupling,
):
    devices = lax.axis_size("leaf")
    position = lax.axis_index("leaf")
    per_dev = leaf_inverse.shape[0]
    leaf_size = leaf_inverse.shape[2]
    rank_size = leaf_basis.shape[2]
    target_count = right_side.shape[0]
    local_levels = per_dev.bit_length() - 1
    cross_levels = devices.bit_length() - 1
    gathered = lax.all_gather(right_side, "rhs", axis=1, tiled=True)
    ordered = jnp.take(gathered, point_order, axis=1).reshape(target_count, per_dev, leaf_size)
    leaf_values = jnp.einsum(
        "slj,lij->lsi", ordered, leaf_inverse, preferred_element_type=jnp.float32
    )
    partial_terms = jnp.einsum(
        "lsi,lik->lsk",
        leaf_values.astype(jnp.bfloat16),
        leaf_basis,
        preferred_element_type=jnp.float32,
    )
    compressed = lax.psum(partial_terms, "rhs").astype(jnp.bfloat16)
    solved_local = []
    for height in range(1, local_levels + 1):
        node_count = per_dev >> height
        offset = per_dev - 2 * node_count
        stacked = jnp.concatenate([compressed[0::2], compressed[1::2]], axis=-1)
        solved = jnp.einsum(
            "nsj,nij->nsi",
            stacked,
            node_inverse[offset : offset + node_count],
            preferred_element_type=jnp.float32,
        )
        solved_local.append(solved)
        partial_terms = jnp.einsum(
            "nsi,nik->nsk",
            solved.astype(jnp.bfloat16),
            node_basis[offset : offset + node_count],
            preferred_element_type=jnp.float32,
        )
        compressed = lax.psum(partial_terms, "rhs").astype(jnp.bfloat16)
    own_inverse = node_inverse[per_dev - 1]
    own_basis = node_basis[per_dev - 1]
    own_coupling = node_coupling[per_dev - 1]
    current = compressed[0]
    solved_cross = []
    for height in range(1, cross_levels + 1):
        distance = 1 if height == 1 else 2 ** (height - 2)
        from_left = fetch_child(current, distance)
        from_right = current if height == 1 else fetch_child(current, -distance)
        stacked = jnp.concatenate([from_left, from_right], axis=-1)
        solved = jnp.einsum("sj,ij->si", stacked, own_inverse, preferred_element_type=jnp.float32)
        solved_cross.append(solved)
        if height < cross_levels:
            partial_terms = jnp.einsum(
                "si,ik->sk",
                solved.astype(jnp.bfloat16),
                own_basis,
                preferred_element_type=jnp.float32,
            )
            current = lax.psum(partial_terms, "rhs").astype(jnp.bfloat16)
    node_value = solved_cross[cross_levels - 1]
    incoming = current
    for height in range(cross_levels, 0, -1):
        shares = node_value.astype(jnp.bfloat16)
        shares = lax.all_gather(shares, "rhs", axis=1, tiled=True)
        distance = 1 if height == 1 else 2 ** (height - 2)
        to_left = send_share(shares[:, :rank_size], -distance)
        to_right = (
            shares[:, rank_size:] if height == 1 else send_share(shares[:, rank_size:], distance)
        )
        is_left = position // 2 ** (height - 1) % 2 == 0
        incoming = jnp.where(is_left, to_left, to_right)
        if height > 1:
            node_value = solved_cross[height - 2] - jnp.einsum(
                "sk,ik->si", incoming, own_coupling, preferred_element_type=jnp.float32
            )
    current = incoming[None]
    for height in range(local_levels, 0, -1):
        node_count = per_dev >> height
        offset = per_dev - 2 * node_count
        node_values = solved_local[height - 1] - jnp.einsum(
            "nsk,nik->nsi",
            current,
            node_coupling[offset : offset + node_count],
            preferred_element_type=jnp.float32,
        )
        shares = lax.all_gather(node_values.astype(jnp.bfloat16), "rhs", axis=2, tiled=True)
        current = jnp.stack([shares[..., :rank_size], shares[..., rank_size:]], axis=1).reshape(
            2 * node_count, target_count, rank_size
        )
    return leaf_values - jnp.einsum(
        "lsk,lik->lsi", current, leaf_coupling, preferred_element_type=jnp.float32
    )


def solution(mesh):
    placed = (
        P(None, ("leaf", "rhs")),
        P("leaf"),
        P("leaf", "rhs", None),
        P("leaf", "rhs", None),
        P("leaf", "rhs", None),
        P("leaf", "rhs", None),
        P("leaf", "rhs", None),
        P("leaf", "rhs", None),
    )
    return jax.shard_map(
        body, mesh=mesh, in_specs=placed, out_specs=P("leaf", None, "rhs"), check_vma=False
    )
```

profile of v0, /device:TPU:256, one launch (start us, length us, event | category | flops | bytes accessed | tf_op | source)
XLA Modules:
  0.0 475.9 jit_solution(10523781956688928829)
XLA Ops:
  0.8 1.1 copy.11
  1.9 14.9 %all_gather.33 = bf16[64,4096]{0,1:T(8,128)(2,1)S(1)} all-gather(bf16[64,1024]{0,1:T(8,128)(2,1)S(1)} %copy.11), channel_id=1, replica_groups=mesh['leaf'=128,'rhs'=4] {'rhs'}, dimensions={1}, use_global_device_ids=true | all-gather | bytes 655360 | tf_op jit(solution)/shard_map/all_gather | solution.py:39
  16.8 12.1 %gather_fusion = bf16[4096,64]{1,0:T(8,128)(2,1)S(1)} fusion(bf16[64,4096]{0,1:T(8,128)(2,1)S(1)} %all_gather.33, s32[4096]{0:T(1024)S(1)} %fusion.135), kind=kCustom, calls=%fused_computation | custom fusion | bytes 1064960 | tf_op jit(solution)/shard_map/jit(_take)/gather | solution.py:40
  30.6 22.2 %all-reduce.3 = bf16[8,64,256]{2,1,0:T(8,128)(2,1)S(1)} all-reduce(f32[8,64,256]{2,1,0:T(8,128)S(1)} %fusion.45), channel_id=1, replica_groups=mesh['leaf'=128,'rhs'=4] {'rhs'}, use_global_device_ids=true, to_apply=%region_0.1 | all-reduce | flops 131072 | bytes 786432 | tf_op jit(solution)/shard_map/psum | solution.py:50
  54.0 18.2 %all-reduce.4 = bf16[4,64,256]{2,1,0:T(8,128)(2,1)S(1)} all-reduce(f32[4,64,256]{2,1,0:T(8,128)S(1)} %fusion.20), channel_id=1, replica_groups=mesh['leaf'=128,'rhs'=4] {'rhs'}, use_global_device_ids=true, to_apply=%region_1.2 | all-reduce | flops 65536 | bytes 393216 | tf_op jit(solution)/shard_map/psum | solution.py:69
  72.3 1.1 fusion.18
  73.6 16.8 %all-reduce.5 = bf16[2,64,256]{2,1,0:T(8,128)(2,1)S(1)} all-reduce(f32[2,64,256]{2,1,0:T(8,128)S(1)} %fusion.43), channel_id=1, replica_groups=mesh['leaf'=128,'rhs'=4] {'rhs'}, use_global_device_ids=true, to_apply=%region_2.3 | all-reduce | flops 32768 | bytes 196608 | tf_op jit(solution)/shard_map/psum | solution.py:69
  91.6 15.6 %psum.73 = bf16[1,64,256]{2,1,0:T(8,128)(2,1)S(1)} all-reduce(f32[1,64,256]{2,1,0:T(8,128)S(1)} %convolution_bitcast_fusion), channel_id=1, replica_groups=mesh['leaf'=128,'rhs'=4] {'rhs'}, use_global_device_ids=true, to_apply=%region_3.4 | all-reduce | flops 16384 | bytes 98304 | tf_op jit(solution)/shard_map/psum | solution.py:69
  107.2 1.9 collective-permute-start
  109.2 6.6 %collective-permute-done = bf16[64,256]{1,0:T(8,128)(2,1)S(1)} collective-permute-done((bf16[64,256]{1,0:T(8,128)(2,1)S(1)}, bf16[64,256]{1,0:T(8,128)(2,1)S(1)}, u32[]{:S(2)}, u32[]{:S(2)}) %collective-permute-start) | collective-permute-done | bytes 32800 | tf_op jit(solution)/shard_map/ppermute | solution.py:10
  117.0 16.1 %psum.74 = bf16[64,256]{1,0:T(8,128)(2,1)S(1)} all-reduce(f32[64,256]{1,0:T(8,128)S(1)} %fusion.89), channel_id=1, replica_groups=mesh['leaf'=128,'rhs'=4] {'rhs'}, use_global_device_ids=true, to_apply=%region_4.5 | all-reduce | flops 16384 | bytes 98304 | tf_op jit(solution)/shard_map/psum | solution.py:89
  133.1 1.9 collective-permute-start.1
  135.0 7.0 %collective-permute-start.2 = (bf16[64,256]{1,0:T(8,128)(2,1)S(1)}, bf16[64,256]{1,0:T(8,128)(2,1)S(1)}, u32[]{:S(2)}, u32[]{:S(2)}) collective-permute-start(bf16[64,256]{1,0:T(8,128)(2,1)S(1)} %psum.74), channel_id=1, source_target_pairs={{4,0},{8,4},{12,8},{16,12},{20,16},{24,20},{28,24},{32,28},{36,32}... | collective-permute-start | bytes 98312 | tf_op jit(solution)/shard_map/ppermute | solution.py:10
  142.0 1.6 collective-permute-done.2
  144.7 15.5 %psum.75 = bf16[64,256]{1,0:T(8,128)(2,1)S(1)} all-reduce(f32[64,256]{1,0:T(8,128)S(1)} %fusion.87), channel_id=1, replica_groups=mesh['leaf'=128,'rhs'=4] {'rhs'}, use_global_device_ids=true, to_apply=%region_5.6 | all-reduce | flops 16384 | bytes 98304 | tf_op jit(solution)/shard_map/psum | solution.py:89
  160.2 1.9 collective-permute-start.3
  162.1 7.2 %collective-permute-start.4 = (bf16[64,256]{1,0:T(8,128)(2,1)S(1)}, bf16[64,256]{1,0:T(8,128)(2,1)S(1)}, u32[]{:S(2)}, u32[]{:S(2)}) collective-permute-start(bf16[64,256]{1,0:T(8,128)(2,1)S(1)} %psum.75), channel_id=1, source_target_pairs={{8,0},{12,4},{16,8},{20,12},{24,16},{28,20},{32,24},{36,28},{40,32... | collective-permute-start | bytes 98312 | tf_op jit(solution)/shard_map/ppermute | solution.py:10
  169.4 1.6 collective-permute-done.4
  172.2 16.1 %psum.76 = bf16[64,256]{1,0:T(8,128)(2,1)S(1)} all-reduce(f32[64,256]{1,0:T(8,128)S(1)} %fusion.85), channel_id=1, replica_groups=mesh['leaf'=128,'rhs'=4] {'rhs'}, use_global_device_ids=true, to_apply=%region_6.7 | all-reduce | flops 16384 | bytes 98304 | tf_op jit(solution)/shard_map/psum | solution.py:89
  188.2 1.9 collective-permute-start.5
  190.2 8.1 %collective-permute-start.6 = (bf16[64,256]{1,0:T(8,128)(2,1)S(1)}, bf16[64,256]{1,0:T(8,128)(2,1)S(1)}, u32[]{:S(2)}, u32[]{:S(2)}) collective-permute-start(bf16[64,256]{1,0:T(8,128)(2,1)S(1)} %psum.76), channel_id=1, source_target_pairs={{16,0},{20,4},{24,8},{28,12},{32,16},{36,20},{40,24},{44,28},{48,3... | collective-permute-start | bytes 98312 | tf_op jit(solution)/shard_map/ppermute | solution.py:10
  198.3 1.6 collective-permute-done.6
  201.1 15.5 %psum.77 = bf16[64,256]{1,0:T(8,128)(2,1)S(1)} all-reduce(f32[64,256]{1,0:T(8,128)S(1)} %fusion.83), channel_id=1, replica_groups=mesh['leaf'=128,'rhs'=4] {'rhs'}, use_global_device_ids=true, to_apply=%region_7.8 | all-reduce | flops 16384 | bytes 98304 | tf_op jit(solution)/shard_map/psum | solution.py:89
  216.6 1.9 collective-permute-start.7
  218.5 9.9 %collective-permute-start.8 = (bf16[64,256]{1,0:T(8,128)(2,1)S(1)}, bf16[64,256]{1,0:T(8,128)(2,1)S(1)}, u32[]{:S(2)}, u32[]{:S(2)}) collective-permute-start(bf16[64,256]{1,0:T(8,128)(2,1)S(1)} %psum.77), channel_id=1, source_target_pairs={{32,0},{36,4},{40,8},{44,12},{48,16},{52,20},{56,24},{60,28},{64,3... | collective-permute-start | bytes 98312 | tf_op jit(solution)/shard_map/ppermute | solution.py:10
  228.5 1.6 collective-permute-done.8
  231.2 16.1 %psum.78 = bf16[64,256]{1,0:T(8,128)(2,1)S(1)} all-reduce(f32[64,256]{1,0:T(8,128)S(1)} %fusion.81), channel_id=1, replica_groups=mesh['leaf'=128,'rhs'=4] {'rhs'}, use_global_device_ids=true, to_apply=%region_8.9 | all-reduce | flops 16384 | bytes 98304 | tf_op jit(solution)/shard_map/psum | solution.py:89
  247.3 3.4 collective-permute-start.10
  250.8 2.5 collective-permute-start.9
  253.3 4.5 collective-permute-done.9
  259.0 15.7 %psum.79 = bf16[64,256]{1,0:T(8,128)(2,1)S(1)} all-reduce(f32[64,256]{1,0:T(8,128)S(1)} %fusion.79), channel_id=1, replica_groups=mesh['leaf'=128,'rhs'=4] {'rhs'}, use_global_device_ids=true, to_apply=%region_9.10 | all-reduce | flops 16384 | bytes 98304 | tf_op jit(solution)/shard_map/psum | solution.py:89
  274.7 1.9 collective-permute-start.11
  276.6 6.0 %collective-permute-start.12 = (bf16[64,256]{1,0:T(8,128)(2,1)S(1)}, bf16[64,256]{1,0:T(8,128)(2,1)S(1)}, u32[]{:S(2)}, u32[]{:S(2)}) collective-permute-start(bf16[64,256]{1,0:T(8,128)(2,1)S(1)} %psum.79), channel_id=1, source_target_pairs={{128,0},{132,4},{136,8},{140,12},{144,16},{148,20},{152,24},{156,2... | collective-permute-start | bytes 98312 | tf_op jit(solution)/shard_map/ppermute | solution.py:10
  282.7 1.6 collective-permute-done.12
  285.3 10.5 %all_gather.34 = bf16[64,512]{1,0:T(8,128)(2,1)S(1)} all-gather(bf16[64,128]{1,0:T(8,128)(2,1)S(1)} %convolution_convert_fusion), channel_id=1, replica_groups=mesh['leaf'=128,'rhs'=4] {'rhs'}, dimensions={1}, use_global_device_ids=true | all-gather | bytes 81920 | tf_op jit(solution)/shard_map/all_gather | solution.py:94
  295.8 6.3 %collective-permute-start.13 = (bf16[64,256]{1,0:T(8,128)(2,1)S(1)}, bf16[64,256]{1,0:T(8,128)(2,1)S(1)}, u32[]{:S(2)}, u32[]{:S(2)}) collective-permute-start(bf16[64,256]{1,0:T(8,128)(2,1)S(1)} %get-tuple-element.26), channel_id=1, source_target_pairs={{128,0},{132,4},{136,8},{140,12},{144,16},{148,20},{152,24},{156,2... | collective-permute-start | bytes 98312 | tf_op jit(solution)/shard_map/ppermute | solution.py:10
  302.1 1.9 collective-permute-start.14
  304.1 5.9 %collective-permute-done.14 = bf16[64,256]{1,0:T(8,128)(2,1)S(1)} collective-permute-done((bf16[64,256]{1,0:T(8,128)(2,1)S(1)}, bf16[64,256]{1,0:T(8,128)(2,1)S(1)}, u32[]{:S(2)}, u32[]{:S(2)}) %collective-permute-start.14) | collective-permute-done | bytes 32800 | tf_op jit(solution)/shard_map/ppermute | solution.py:10
  310.1 10.5 %all_gather.35 = bf16[64,512]{1,0:T(8,128)(2,1)S(1)} all-gather(bf16[64,128]{1,0:T(8,128)(2,1)S(1)} %fusion.2), channel_id=1, replica_groups=mesh['leaf'=128,'rhs'=4] {'rhs'}, dimensions={1}, use_global_device_ids=true | all-gather | bytes 81920 | tf_op jit(solution)/shard_map/all_gather | solution.py:94
  320.7 1.9 collective-permute-start.15
  322.6 3.9 collective-permute-start.16
  326.6 3.0 collective-permute-done.16
  329.7 10.5 %all_gather.36 = bf16[64,512]{1,0:T(8,128)(2,1)S(1)} all-gather(bf16[64,128]{1,0:T(8,128)(2,1)S(1)} %fusion.3), channel_id=1, replica_groups=mesh['leaf'=128,'rhs'=4] {'rhs'}, dimensions={1}, use_global_device_ids=true | all-gather | bytes 81920 | tf_op jit(solution)/shard_map/all_gather | solution.py:94
  340.2 8.4 %collective-permute-start.17 = (bf16[64,256]{1,0:T(8,128)(2,1)S(1)}, bf16[64,256]{1,0:T(8,128)(2,1)S(1)}, u32[]{:S(2)}, u32[]{:S(2)}) collective-permute-start(bf16[64,256]{1,0:T(8,128)(2,1)S(1)} %get-tuple-element.22), channel_id=1, source_target_pairs={{32,0},{36,4},{40,8},{44,12},{48,16},{52,20},{56,24},{60,28},{64,3... | collective-permute-start | bytes 98312 | tf_op jit(solution)/shard_map/ppermute | solution.py:10
  348.7 2.8 collective-permute-start.18
  351.5 9.5 %collective-permute-done.18 = bf16[64,256]{1,0:T(8,128)(2,1)S(1)} collective-permute-done((bf16[64,256]{1,0:T(8,128)(2,1)S(1)}, bf16[64,256]{1,0:T(8,128)(2,1)S(1)}, u32[]{:S(2)}, u32[]{:S(2)}) %collective-permute-start.18) | collective-permute-done | bytes 32800 | tf_op jit(solution)/shard_map/ppermute | solution.py:10
  361.2 10.5 %all_gather.37 = bf16[64,512]{1,0:T(8,128)(2,1)S(1)} all-gather(bf16[64,128]{1,0:T(8,128)(2,1)S(1)} %fusion.4), channel_id=1, replica_groups=mesh['leaf'=128,'rhs'=4] {'rhs'}, dimensions={1}, use_global_device_ids=true | all-gather | bytes 81920 | tf_op jit(solution)/shard_map/all_gather | solution.py:94
  371.7 1.9 collective-permute-start.19
  373.6 4.8 %collective-permute-start.20 = (bf16[64,256]{1,0:T(8,128)(2,1)S(1)}, bf16[64,256]{1,0:T(8,128)(2,1)S(1)}, u32[]{:S(2)}, u32[]{:S(2)}) collective-permute-start(bf16[64,256]{1,0:T(8,128)(2,1)S(1)} %get-tuple-element.19), channel_id=1, source_target_pairs={{0,16},{4,20},{8,24},{12,28},{16,32},{20,36},{24,40},{28,44},{32,4... | collective-permute-start | bytes 98312 | tf_op jit(solution)/shard_map/ppermute | solution.py:10
  378.4 5.2 %collective-permute-done.20 = bf16[64,256]{1,0:T(8,128)(2,1)S(1)} collective-permute-done((bf16[64,256]{1,0:T(8,128)(2,1)S(1)}, bf16[64,256]{1,0:T(8,128)(2,1)S(1)}, u32[]{:S(2)}, u32[]{:S(2)}) %collective-permute-start.20) | collective-permute-done | bytes 32800 | tf_op jit(solution)/shard_map/ppermute | solution.py:10
  383.7 10.5 %all_gather.38 = bf16[64,512]{1,0:T(8,128)(2,1)S(1)} all-gather(bf16[64,128]{1,0:T(8,128)(2,1)S(1)} %fusion.5), channel_id=1, replica_groups=mesh['leaf'=128,'rhs'=4] {'rhs'}, dimensions={1}, use_global_device_ids=true | all-gather | bytes 81920 | tf_op jit(solution)/shard_map/all_gather | solution.py:94
  394.3 1.9 collective-permute-start.21
  396.2 3.9 collective-permute-start.22
  400.1 5.2 %collective-permute-done.22 = bf16[64,256]{1,0:T(8,128)(2,1)S(1)} collective-permute-done((bf16[64,256]{1,0:T(8,128)(2,1)S(1)}, bf16[64,256]{1,0:T(8,128)(2,1)S(1)}, u32[]{:S(2)}, u32[]{:S(2)}) %collective-permute-start.22) | collective-permute-done | bytes 32800 | tf_op jit(solution)/shard_map/ppermute | solution.py:10
  405.4 10.5 %all_gather.39 = bf16[64,512]{1,0:T(8,128)(2,1)S(1)} all-gather(bf16[64,128]{1,0:T(8,128)(2,1)S(1)} %fusion.6), channel_id=1, replica_groups=mesh['leaf'=128,'rhs'=4] {'rhs'}, dimensions={1}, use_global_device_ids=true | all-gather | bytes 81920 | tf_op jit(solution)/shard_map/all_gather | solution.py:94
  415.9 1.9 collective-permute-start.23
  417.8 2.4 collective-permute-start.24
  420.3 6.1 %collective-permute-done.24 = bf16[64,256]{1,0:T(8,128)(2,1)S(1)} collective-permute-done((bf16[64,256]{1,0:T(8,128)(2,1)S(1)}, bf16[64,256]{1,0:T(8,128)(2,1)S(1)}, u32[]{:S(2)}, u32[]{:S(2)}) %collective-permute-start.24) | collective-permute-done | bytes 32800 | tf_op jit(solution)/shard_map/ppermute | solution.py:10
  426.5 10.5 %all_gather.40 = bf16[64,512]{1,0:T(8,128)(2,1)S(1)} all-gather(bf16[64,128]{1,0:T(8,128)(2,1)S(1)} %fusion.7), channel_id=1, replica_groups=mesh['leaf'=128,'rhs'=4] {'rhs'}, dimensions={1}, use_global_device_ids=true | all-gather | bytes 81920 | tf_op jit(solution)/shard_map/all_gather | solution.py:94
  437.0 1.9 collective-permute-start.25
  439.0 1.6 collective-permute-done.25
  440.7 10.5 %all-gather = bf16[64,512]{1,0:T(8,128)(2,1)S(1)} all-gather(bf16[64,128]{1,0:T(8,128)(2,1)S(1)} %fusion.8), channel_id=2, replica_groups=mesh['leaf'=128,'rhs'=4] {'rhs'}, dimensions={1}, use_global_device_ids=true | all-gather | bytes 81920 | tf_op jit(solution)/shard_map/all_gather | solution.py:116
  451.3 10.8 %all_gather.42 = bf16[2,64,512]{2,1,0:T(8,128)(2,1)S(1)} all-gather(bf16[2,64,128]{2,1,0:T(8,128)(2,1)S(1)} %fusion.1), channel_id=1, replica_groups=mesh['leaf'=128,'rhs'=4] {'rhs'}, dimensions={2}, use_global_device_ids=true | all-gather | bytes 163840 | tf_op jit(solution)/shard_map/all_gather | solution.py:116
  462.4 11.5 %all_gather.43 = bf16[4,64,512]{2,1,0:T(8,128)(2,1)S(1)} all-gather(bf16[4,64,128]{2,1,0:T(8,128)(2,1)S(1)} %fusion), channel_id=1, replica_groups=mesh['leaf'=128,'rhs'=4] {'rhs'}, dimensions={2}, use_global_device_ids=true | all-gather | bytes 327680 | tf_op jit(solution)/shard_map/all_gather | solution.py:116
  (77 shorter events, 16.7 us)
Async XLA Ops:
  0.0 29.3 %copy-start = (bf16[8,128,512]{2,1,0:T(8,128)(2,1)S(1)}, bf16[8,128,512]{2,1,0:T(8,128)(2,1)}, u32[]{:S(2)}) copy-start(bf16[8,128,512]{2,1,0:T(8,128)(2,1)} %param.10) | copy-start | bytes 3145732
  0.0 0.8 copy-start.5
  29.3 1.0 copy-start.3
  30.3 22.4 %copy-start.6 = (bf16[8,128,512]{2,1,0:T(8,128)(2,1)S(1)}, bf16[8,128,512]{2,1,0:T(8,128)(2,1)}, u32[]{:S(2)}) copy-start(bf16[8,128,512]{2,1,0:T(8,128)(2,1)} %param.13) | copy-start | bytes 3145732
  52.8 1.0 copy-start.1
  107.2 8.6 %collective-permute-start = (bf16[64,256]{1,0:T(8,128)(2,1)S(1)}, bf16[64,256]{1,0:T(8,128)(2,1)S(1)}, u32[]{:S(2)}, u32[]{:S(2)}) collective-permute-start(bf16[64,256]{1,0:T(8,128)(2,1)S(1)} %bitcast.88), channel_id=1, source_target_pairs={{0,4},{4,8},{8,12},{12,16},{16,20},{20,24},{24,28},{28,32},{32,36}... | collective-permute-start | bytes 98312 | tf_op jit(solution)/shard_map/ppermute | solution.py:10
  133.1 8.9 %collective-permute-start.1 = (bf16[64,256]{1,0:T(8,128)(2,1)S(1)}, bf16[64,256]{1,0:T(8,128)(2,1)S(1)}, u32[]{:S(2)}, u32[]{:S(2)}) collective-permute-start(bf16[64,256]{1,0:T(8,128)(2,1)S(1)} %psum.74), channel_id=1, source_target_pairs={{0,4},{4,8},{8,12},{12,16},{16,20},{20,24},{24,28},{28,32},{32,36}... | collective-permute-start | bytes 98312 | tf_op jit(solution)/shard_map/ppermute | solution.py:10
  135.0 8.5 %collective-permute-start.2 = (bf16[64,256]{1,0:T(8,128)(2,1)S(1)}, bf16[64,256]{1,0:T(8,128)(2,1)S(1)}, u32[]{:S(2)}, u32[]{:S(2)}) collective-permute-start(bf16[64,256]{1,0:T(8,128)(2,1)S(1)} %psum.74), channel_id=1, source_target_pairs={{4,0},{8,4},{12,8},{16,12},{20,16},{24,20},{28,24},{32,28},{36,32}... | collective-permute-start | bytes 98312 | tf_op jit(solution)/shard_map/ppermute | solution.py:10
  160.2 9.2 %collective-permute-start.3 = (bf16[64,256]{1,0:T(8,128)(2,1)S(1)}, bf16[64,256]{1,0:T(8,128)(2,1)S(1)}, u32[]{:S(2)}, u32[]{:S(2)}) collective-permute-start(bf16[64,256]{1,0:T(8,128)(2,1)S(1)} %psum.75), channel_id=1, source_target_pairs={{0,8},{4,12},{8,16},{12,20},{16,24},{20,28},{24,32},{28,36},{32,40... | collective-permute-start | bytes 98312 | tf_op jit(solution)/shard_map/ppermute | solution.py:10
  162.1 8.8 %collective-permute-start.4 = (bf16[64,256]{1,0:T(8,128)(2,1)S(1)}, bf16[64,256]{1,0:T(8,128)(2,1)S(1)}, u32[]{:S(2)}, u32[]{:S(2)}) collective-permute-start(bf16[64,256]{1,0:T(8,128)(2,1)S(1)} %psum.75), channel_id=1, source_target_pairs={{8,0},{12,4},{16,8},{20,12},{24,16},{28,20},{32,24},{36,28},{40,32... | collective-permute-start | bytes 98312 | tf_op jit(solution)/shard_map/ppermute | solution.py:10
  188.2 10.1 %collective-permute-start.5 = (bf16[64,256]{1,0:T(8,128)(2,1)S(1)}, bf16[64,256]{1,0:T(8,128)(2,1)S(1)}, u32[]{:S(2)}, u32[]{:S(2)}) collective-permute-start(bf16[64,256]{1,0:T(8,128)(2,1)S(1)} %psum.76), channel_id=1, source_target_pairs={{0,16},{4,20},{8,24},{12,28},{16,32},{20,36},{24,40},{28,44},{32,4... | collective-permute-start | bytes 98312 | tf_op jit(solution)/shard_map/ppermute | solution.py:10
  190.2 9.7 %collective-permute-start.6 = (bf16[64,256]{1,0:T(8,128)(2,1)S(1)}, bf16[64,256]{1,0:T(8,128)(2,1)S(1)}, u32[]{:S(2)}, u32[]{:S(2)}) collective-permute-start(bf16[64,256]{1,0:T(8,128)(2,1)S(1)} %psum.76), channel_id=1, source_target_pairs={{16,0},{20,4},{24,8},{28,12},{32,16},{36,20},{40,24},{44,28},{48,3... | collective-permute-start | bytes 98312 | tf_op jit(solution)/shard_map/ppermute | solution.py:10
  216.6 11.9 %collective-permute-start.7 = (bf16[64,256]{1,0:T(8,128)(2,1)S(1)}, bf16[64,256]{1,0:T(8,128)(2,1)S(1)}, u32[]{:S(2)}, u32[]{:S(2)}) collective-permute-start(bf16[64,256]{1,0:T(8,128)(2,1)S(1)} %psum.77), channel_id=1, source_target_pairs={{0,32},{4,36},{8,40},{12,44},{16,48},{20,52},{24,56},{28,60},{32,6... | collective-permute-start | bytes 98312 | tf_op jit(solution)/shard_map/ppermute | solution.py:10
  218.5 11.5 %collective-permute-start.8 = (bf16[64,256]{1,0:T(8,128)(2,1)S(1)}, bf16[64,256]{1,0:T(8,128)(2,1)S(1)}, u32[]{:S(2)}, u32[]{:S(2)}) collective-permute-start(bf16[64,256]{1,0:T(8,128)(2,1)S(1)} %psum.77), channel_id=1, source_target_pairs={{32,0},{36,4},{40,8},{44,12},{48,16},{52,20},{56,24},{60,28},{64,3... | collective-permute-start | bytes 98312 | tf_op jit(solution)/shard_map/ppermute | solution.py:10
  247.3 62.7 %copy-start.2 = (bf16[8,128,256]{2,1,0:T(8,128)(2,1)S(1)}, bf16[8,128,256]{2,1,0:T(8,128)(2,1)}, u32[]{:S(2)}) copy-start(bf16[8,128,256]{2,1,0:T(8,128)(2,1)} %param.15) | copy-start | bytes 1572868
  247.3 6.0 %collective-permute-start.10 = (bf16[64,256]{1,0:T(8,128)(2,1)S(1)}, bf16[64,256]{1,0:T(8,128)(2,1)S(1)}, u32[]{:S(2)}, u32[]{:S(2)}) collective-permute-start(bf16[64,256]{1,0:T(8,128)(2,1)S(1)} %psum.78), channel_id=1, source_target_pairs={{64,0},{68,4},{72,8},{76,12},{80,16},{84,20},{88,24},{92,28},{96,3... | collective-permute-start | bytes 98312 | tf_op jit(solution)/shard_map/ppermute | solution.py:10
  250.8 7.0 %collective-permute-start.9 = (bf16[64,256]{1,0:T(8,128)(2,1)S(1)}, bf16[64,256]{1,0:T(8,128)(2,1)S(1)}, u32[]{:S(2)}, u32[]{:S(2)}) collective-permute-start(bf16[64,256]{1,0:T(8,128)(2,1)S(1)} %psum.78), channel_id=1, source_target_pairs={{0,64},{4,68},{8,72},{12,76},{16,80},{20,84},{24,88},{28,92},{32,9... | collective-permute-start | bytes 98312 | tf_op jit(solution)/shard_map/ppermute | solution.py:10
  274.7 8.0 %collective-permute-start.11 = (bf16[64,256]{1,0:T(8,128)(2,1)S(1)}, bf16[64,256]{1,0:T(8,128)(2,1)S(1)}, u32[]{:S(2)}, u32[]{:S(2)}) collective-permute-start(bf16[64,256]{1,0:T(8,128)(2,1)S(1)} %psum.79), channel_id=1, source_target_pairs={{0,128},{4,132},{8,136},{12,140},{16,144},{20,148},{24,152},{28,15... | collective-permute-start | bytes 98312 | tf_op jit(solution)/shard_map/ppermute | solution.py:10
  276.6 7.6 %collective-permute-start.12 = (bf16[64,256]{1,0:T(8,128)(2,1)S(1)}, bf16[64,256]{1,0:T(8,128)(2,1)S(1)}, u32[]{:S(2)}, u32[]{:S(2)}) collective-permute-start(bf16[64,256]{1,0:T(8,128)(2,1)S(1)} %psum.79), channel_id=1, source_target_pairs={{128,0},{132,4},{136,8},{140,12},{144,16},{148,20},{152,24},{156,2... | collective-permute-start | bytes 98312 | tf_op jit(solution)/shard_map/ppermute | solution.py:10
  295.8 8.3 %collective-permute-start.13 = (bf16[64,256]{1,0:T(8,128)(2,1)S(1)}, bf16[64,256]{1,0:T(8,128)(2,1)S(1)}, u32[]{:S(2)}, u32[]{:S(2)}) collective-permute-start(bf16[64,256]{1,0:T(8,128)(2,1)S(1)} %get-tuple-element.26), channel_id=1, source_target_pairs={{128,0},{132,4},{136,8},{140,12},{144,16},{148,20},{152,24},{156,2... | collective-permute-start | bytes 98312 | tf_op jit(solution)/shard_map/ppermute | solution.py:10
  302.1 7.9 %collective-permute-start.14 = (bf16[64,256]{1,0:T(8,128)(2,1)S(1)}, bf16[64,256]{1,0:T(8,128)(2,1)S(1)}, u32[]{:S(2)}, u32[]{:S(2)}) collective-permute-start(bf16[64,256]{1,0:T(8,128)(2,1)S(1)} %get-tuple-element.25), channel_id=1, source_target_pairs={{0,128},{4,132},{8,136},{12,140},{16,144},{20,148},{24,152},{28,15... | collective-permute-start | bytes 98312 | tf_op jit(solution)/shard_map/ppermute | solution.py:10
  320.7 5.9 %collective-permute-start.15 = (bf16[64,256]{1,0:T(8,128)(2,1)S(1)}, bf16[64,256]{1,0:T(8,128)(2,1)S(1)}, u32[]{:S(2)}, u32[]{:S(2)}) collective-permute-start(bf16[64,256]{1,0:T(8,128)(2,1)S(1)} %get-tuple-element.24), channel_id=1, source_target_pairs={{64,0},{68,4},{72,8},{76,12},{80,16},{84,20},{88,24},{92,28},{96,3... | collective-permute-start | bytes 98312 | tf_op jit(solution)/shard_map/ppermute | solution.py:10
  322.6 7.0 %collective-permute-start.16 = (bf16[64,256]{1,0:T(8,128)(2,1)S(1)}, bf16[64,256]{1,0:T(8,128)(2,1)S(1)}, u32[]{:S(2)}, u32[]{:S(2)}) collective-permute-start(bf16[64,256]{1,0:T(8,128)(2,1)S(1)} %get-tuple-element.23), channel_id=1, source_target_pairs={{0,64},{4,68},{8,72},{12,76},{16,80},{20,84},{24,88},{28,92},{32,9... | collective-permute-start | bytes 98312 | tf_op jit(solution)/shard_map/ppermute | solution.py:10
  340.2 11.3 %collective-permute-start.17 = (bf16[64,256]{1,0:T(8,128)(2,1)S(1)}, bf16[64,256]{1,0:T(8,128)(2,1)S(1)}, u32[]{:S(2)}, u32[]{:S(2)}) collective-permute-start(bf16[64,256]{1,0:T(8,128)(2,1)S(1)} %get-tuple-element.22), channel_id=1, source_target_pairs={{32,0},{36,4},{40,8},{44,12},{48,16},{52,20},{56,24},{60,28},{64,3... | collective-permute-start | bytes 98312 | tf_op jit(solution)/shard_map/ppermute | solution.py:10
  348.7 12.3 %collective-permute-start.18 = (bf16[64,256]{1,0:T(8,128)(2,1)S(1)}, bf16[64,256]{1,0:T(8,128)(2,1)S(1)}, u32[]{:S(2)}, u32[]{:S(2)}) collective-permute-start(bf16[64,256]{1,0:T(8,128)(2,1)S(1)} %get-tuple-element.21), channel_id=1, source_target_pairs={{0,32},{4,36},{8,40},{12,44},{16,48},{20,52},{24,56},{28,60},{32,6... | collective-permute-start | bytes 98312 | tf_op jit(solution)/shard_map/ppermute | solution.py:10
  371.7 6.8 %collective-permute-start.19 = (bf16[64,256]{1,0:T(8,128)(2,1)S(1)}, bf16[64,256]{1,0:T(8,128)(2,1)S(1)}, u32[]{:S(2)}, u32[]{:S(2)}) collective-permute-start(bf16[64,256]{1,0:T(8,128)(2,1)S(1)} %get-tuple-element.20), channel_id=1, source_target_pairs={{16,0},{20,4},{24,8},{28,12},{32,16},{36,20},{40,24},{44,28},{48,3... | collective-permute-start | bytes 98312 | tf_op jit(solution)/shard_map/ppermute | solution.py:10
  373.6 10.0 %collective-permute-start.20 = (bf16[64,256]{1,0:T(8,128)(2,1)S(1)}, bf16[64,256]{1,0:T(8,128)(2,1)S(1)}, u32[]{:S(2)}, u32[]{:S(2)}) collective-permute-start(bf16[64,256]{1,0:T(8,128)(2,1)S(1)} %get-tuple-element.19), channel_id=1, source_target_pairs={{0,16},{4,20},{8,24},{12,28},{16,32},{20,36},{24,40},{28,44},{32,4... | collective-permute-start | bytes 98312 | tf_op jit(solution)/shard_map/ppermute | solution.py:10
  394.3 5.9 %collective-permute-start.21 = (bf16[64,256]{1,0:T(8,128)(2,1)S(1)}, bf16[64,256]{1,0:T(8,128)(2,1)S(1)}, u32[]{:S(2)}, u32[]{:S(2)}) collective-permute-start(bf16[64,256]{1,0:T(8,128)(2,1)S(1)} %get-tuple-element.18), channel_id=1, source_target_pairs={{8,0},{12,4},{16,8},{20,12},{24,16},{28,20},{32,24},{36,28},{40,32... | collective-permute-start | bytes 98312 | tf_op jit(solution)/shard_map/ppermute | solution.py:10
  396.2 9.1 %collective-permute-start.22 = (bf16[64,256]{1,0:T(8,128)(2,1)S(1)}, bf16[64,256]{1,0:T(8,128)(2,1)S(1)}, u32[]{:S(2)}, u32[]{:S(2)}) collective-permute-start(bf16[64,256]{1,0:T(8,128)(2,1)S(1)} %get-tuple-element.17), channel_id=1, source_target_pairs={{0,8},{4,12},{8,16},{12,20},{16,24},{20,28},{24,32},{28,36},{32,40... | collective-permute-start | bytes 98312 | tf_op jit(solution)/shard_map/ppermute | solution.py:10
  415.9 4.4 collective-permute-start.23
  417.8 8.6 %collective-permute-start.24 = (bf16[64,256]{1,0:T(8,128)(2,1)S(1)}, bf16[64,256]{1,0:T(8,128)(2,1)S(1)}, u32[]{:S(2)}, u32[]{:S(2)}) collective-permute-start(bf16[64,256]{1,0:T(8,128)(2,1)S(1)} %get-tuple-element.15), channel_id=1, source_target_pairs={{0,4},{4,8},{8,12},{12,16},{16,20},{20,24},{24,28},{28,32},{32,36}... | collective-permute-start | bytes 98312 | tf_op jit(solution)/shard_map/ppermute | solution.py:10
  437.0 3.5 collective-permute-start.25
  473.9 1.0 copy-start.4
where the time goes:
time: 477 us; the launch traced here: 476 us
  blocking collectives  289 us (61%)
  starting transfers between devices  99.9 us (21%)
  waiting for transfers between devices  55.5 us (12%)
  local copies, waits for them, and re-layouts  16 us (3%)
  matrix products  14.2 us (3%)
    ppermute x26, starting transfers between devices, from_behind(): return lax.ppermute(block, axis, route)  99.9 us
    psum x6, blocking collectives, body(): current = lax.psum(partial_terms, 'rhs').astype(jnp.bfloat16)  94.8 us
    all_gather x7, blocking collectives, body(): shares = lax.all_gather(shares, 'rhs', axis=1, tiled=True)  73.5 us
    psum x4, blocking collectives, body(): compressed = lax.psum(partial_terms, 'rhs').astype(jnp.bfloat16)  72.8 us
    ppermute x26, waiting for transfers between devices, from_behind(): return lax.ppermute(block, axis, route)  55.5 us
    all_gather x3, blocking collectives, body(): lax.all_gather(node_values.astype(jnp.bfloat16), 'rhs', axis=2, tiled=True)  32.7 us
    all_gather x1, blocking collectives, body(): gathered = lax.all_gather(right_side, 'rhs', axis=1, tiled=True)  14.9 us
    gather x2, local copies, waits for them, and re-layouts, body(): jnp.take(gathered, point_order, axis=1)  12.5 us
  transfers between devices with their start and end apart: 26, of which 14 were waited for; matrix products, arithmetic and copies ran while one was open for 0% of the time, Pallas kernels for 0%

commit v1 on v0

v1 whole, which is shorter than its diff:
```python
import jax
import jax.numpy as jnp
from jax import lax
from jax.experimental import pallas as pl
from jax.experimental.pallas import tpu as pltpu
from jax.sharding import PartitionSpec as P

MESH = pl.DeviceIdType.MESH
BF = jnp.bfloat16
F32 = jnp.float32
VMEM = pltpu.VMEM


def nt(a, b):
    return lax.dot_general(a, b, (((1,), (1,)), ((), ())), preferred_element_type=F32)


def nn(a, b):
    return lax.dot_general(a, b, (((1,), (0,)), ((), ())), preferred_element_type=F32)


def xor(a, k):
    total = 0
    for bit in (1, 2):
        digit = (a // bit) % 2
        total = total + bit * ((1 - digit) if k & bit else digit)
    return total


def when(cond):
    return pl.when(cond)


N_SEMS = 96


def kernel(
    rs, po, linv, lbas, lcou, ninv, nbas, ncou, out,
    tg, acc, lv, linv_v, lbas_v, lcou_v, ninv_v, nbas_v, ncou_v,
    rsb, rsr, c0g, p1, p1r, c1, p2, p2r, c2, p3, p3r, c3, c3l,
    s1, s2, s3, finv, fbas, fcou, fs, cs, up2, up3, up4, up5, up6, up7,
    vb, db, incg, d3, d2, d1,
    lsem, ssem, rsem, fss, frs,
):
    leaf = lax.axis_index("leaf")
    x = lax.axis_index("rhs")
    core = leaf % 2
    y = (leaf // 2) % 8
    z = leaf // 16

    def at(z_, y_, c_, x_):
        return ((z_ * 8 + y_) * 2 + c_, x_)

    counter = [0]
    pending = []

    def remote(src, dst, target, my_dst=None, cond=None, lands=None):
        i = counter[0]
        counter[0] += 1
        j = i if lands is None else lands
        send = pltpu.make_async_remote_copy(
            src_ref=src, dst_ref=dst, send_sem=ssem.at[i], recv_sem=rsem.at[j],
            device_id=target, device_id_type=MESH,
        )
        here = dst if my_dst is None else my_dst
        recv = pltpu.make_async_remote_copy(
            src_ref=src, dst_ref=here, send_sem=ssem.at[i], recv_sem=rsem.at[j],
            device_id=target, device_id_type=MESH,
        )
        pending.append((cond, send))
        return send, recv

    local = [
        pltpu.make_async_copy(src, dst, lsem.at[i])
        for i, (src, dst) in enumerate(
            (
                (linv, linv_v), (lbas, lbas_v),
                (ninv.at[pl.ds(0, 7)], ninv_v), (nbas.at[pl.ds(0, 7)], nbas_v),
                (ncou.at[pl.ds(0, 7)], ncou_v), (lcou, lcou_v),
            )
        )
    ]
    for copy in local:
        copy.start()

    xs = [xor(x, k) for k in range(4)]
    is0 = core == 0
    is1 = core == 1
    y_odd = y % 2 == 1
    y_mid = y % 4 == 2
    z_odd = z % 2 == 1
    z_mid = z % 4 == 2
    y_pair = y + 1 - 2 * (y % 2)
    z_pair = z + 1 - 2 * (z % 2)
    y_own = (y // 4) * 4 + 2
    z_own = (z // 4) * 4 + 2
    row1 = is1 & (y == 0)
    moved = is0 & (y == 4)
    y_to = jnp.where(moved, 0, y)

    barrier = pltpu.get_barrier_semaphore()

    def greet(*target):
        pl.semaphore_signal(barrier, inc=1, device_id=at(*target), device_id_type=MESH)

    def greet_if(cond, *targets):
        @when(cond)
        def _():
            for target in targets:
                greet(*target)

    def as_int(cond):
        return jnp.where(cond, 1, 0)

    for k in (1, 2, 3):
        greet(z, y, core, xs[k])
    greet(z, y, 1 - core, x)
    greet_if(is1 & (y != 4), *[(z, y, 0, xs[k]) for k in (1, 2, 3)])
    greet_if(row1, *[(z, 4, 0, xs[k]) for k in range(4)])
    greet_if(is1, (z, y_pair, 1, x))
    greet_if(is1 & y_odd, (z, y_own, 1, x))
    greet_if(is1 & y_mid, (z, y - 1, 1, x), (z, y + 1, 1, x), (z, 0, 1, x))
    greet_if(row1, (z, 2, 1, x), (z, 6, 1, x), (z_pair, 0, 1, x))
    greet_if(row1 & z_odd, (z_own, 0, 1, x))
    greet_if(row1 & z_mid, (z - 1, 0, 1, x), (z + 1, 0, 1, x), (4, 0, 1, x))
    greet_if(row1 & (z == 4), (2, 0, 1, x), (6, 0, 1, x))
    expect = (
        4
        + as_int(is0) * 3
        + as_int(moved)
        + as_int(is1)
        + as_int(is1 & y_odd)
        + as_int(is1 & y_mid) * 3
        + as_int(row1) * 3
        + as_int(row1 & z_odd)
        + as_int(row1 & z_mid) * 3
        + as_int(row1 & (z == 4)) * 2
    )
    pl.semaphore_wait(barrier, expect)

    gather = [
        remote(rs, tg.at[k - 1], at(z, y, core, xs[k])) for k in (1, 3, 2)
    ]
    for send, _ in gather:
        send.start()

    slot = jnp.where(is1, 0, jnp.where(moved, 2, 1))
    factors = ((ninv.at[7], finv), (nbas.at[7], fbas), (ncou.at[7], fcou))

    def factor_copy(which, k):
        src, dst = factors[which]
        return pltpu.make_async_remote_copy(
            src_ref=src, dst_ref=dst.at[slot, x], send_sem=fss.at[which, k],
            recv_sem=frs.at[which, slot, k], device_id=at(z, y_to, 1, xs[k]), device_id_type=MESH,
        )

    def factor_own(which):
        src, dst = factors[which]
        return pltpu.make_async_copy(src, dst.at[0, x], fss.at[which, 0])

    def send_factors(which):
        for k in (1, 3, 2):
            factor_copy(which, k).start()

        @when(is0)
        def _():
            factor_copy(which, 0).start()

        @when(is1)
        def _():
            factor_own(which).start()

    def wait_factors(which, place):
        src, dst = factors[which]
        for k in range(4):
            if place == 0 and k == 0:
                factor_own(which).wait()
                continue
            pltpu.make_async_remote_copy(
                src_ref=src, dst_ref=dst.at[place, xs[k]], send_sem=fss.at[which, k],
                recv_sem=frs.at[which, place, k], device_id=at(z, y, 0, xs[k]), device_id_type=MESH,
            ).wait_recv()

    wide = 512

    def permute(block, source, first):
        base = source * 1024

        def part(j, carry):
            cols = pl.ds(pl.multiple_of(j * wide, wide), wide)
            rows = lax.broadcasted_iota(jnp.int32, (1024, wide), 0) + base
            hot = jnp.where(rows == po[:, cols], 1.0, 0.0).astype(BF)
            term = nn(block, hot)
            acc[:, cols] = term if first else acc[:, cols] + term
            return carry

        lax.fori_loop(0, 4096 // wide, part, 0)

    permute(rs[...], x, True)
    for (_, recv), k in zip(gather, (1, 3, 2)):
        recv.wait_recv()
        permute(tg[k - 1], xs[k], False)

    local[0].wait()
    local[1].wait()
    for l in range(8):
        value = nt(acc[:, l * 512 : (l + 1) * 512].astype(BF), linv_v[l])
        lv[l] = value
        part = nn(value.astype(BF), lbas_v[l]).astype(BF)
        for q in range(4):
            rsb[q, l] = part[16 * q : 16 * q + 16]

    scatter = [remote(rsb.at[xs[k]], rsr.at[k - 1], at(z, y, core, xs[k])) for k in (1, 3, 2)]
    for send, _ in scatter:
        send.start()
    send_factors(0)
    for _, recv in scatter:
        recv.wait_recv()
    total = rsb[x].astype(F32)
    for k in range(3):
        total = total + rsr[k].astype(F32)
    c0g[x] = total.astype(BF)

    def spread(buffer):
        copies = [
            remote(buffer.at[x], buffer.at[x], at(z, y, core, xs[k]), my_dst=buffer.at[xs[k]])
            for k in (1, 3, 2)
        ]
        for send, _ in copies:
            send.start()
        return [recv for _, recv in copies]

    for recv in spread(c0g):
        recv.wait_recv()

    local[2].wait()
    local[3].wait()

    def exchange(src, dst):
        copies = [remote(src, dst.at[k - 1], at(z, y, core, xs[k])) for k in (1, 3, 2)]
        for send, _ in copies:
            send.start()
        return [recv for _, recv in copies]

    for n in range(4):
        left = c0g[:, 2 * n].reshape(64, 256)
        right = c0g[:, 2 * n + 1].reshape(64, 256)
        solved = nt(jnp.concatenate([left, right], axis=1), ninv_v[n])
        s1[n] = solved
        p1[n] = nn(solved.astype(BF), nbas_v[n]).astype(BF)
    recvs = exchange(p1, p1r)
    send_factors(1)
    for recv in recvs:
        recv.wait_recv()
    for n in range(4):
        total = p1[n].astype(F32)
        for k in range(3):
            total = total + p1r[k, n].astype(F32)
        c1[n] = total.astype(BF)

    for n in range(2):
        solved = nt(jnp.concatenate([c1[2 * n], c1[2 * n + 1]], axis=1), ninv_v[4 + n])
        s2[n] = solved
        p2[n] = nn(solved.astype(BF), nbas_v[4 + n]).astype(BF)
    recvs = exchange(p2, p2r)
    send_factors(2)
    for recv in recvs:
        recv.wait_recv()
    for n in range(2):
        total = p2[n].astype(F32)
        for k in range(3):
            total = total + p2r[k, n].astype(F32)
        c2[n] = total.astype(BF)

    solved = nt(jnp.concatenate([c2[0], c2[1]], axis=1), ninv_v[6])
    s3[...] = solved
    part = nn(solved.astype(BF), nbas_v[6]).astype(BF)
    for q in range(4):
        p3[q] = part[16 * q : 16 * q + 16]
    scatter = [remote(p3.at[xs[k]], p3r.at[k - 1], at(z, y, core, xs[k])) for k in (1, 3, 2)]
    for send, _ in scatter:
        send.start()
    for _, recv in scatter:
        recv.wait_recv()
    total = p3[x].astype(F32)
    for k in range(3):
        total = total + p3r[k].astype(F32)
    c3[...] = total.astype(BF)

    def up(place, left, right):
        wait_factors(0, place)
        wait_factors(1, place)
        solved = nt(jnp.concatenate([left, right], axis=1), finv[place].reshape(512, 512))
        fs[place] = solved
        return nn(solved.astype(BF), fbas[place].reshape(512, 256)).astype(BF)

    def down(place, h):
        wait_factors(2, place)
        value = (fs[place] - nt(db[h], fcou[place].reshape(512, 256))).astype(BF)
        vb[h, 0] = value[:, :256]
        vb[h, 1] = value[:, 256:]

    core_up, core_up_recv = remote(c3, c3l, at(z, y, 1, x), cond=is0)
    core_down, core_down_recv = remote(vb.at[1, 0], db.at[0], at(z, y, 0, x), cond=is1)
    y_even = is1 & (y % 2 == 0)
    row_even = row1 & (z % 2 == 0)
    odd1 = is1 & y_odd
    mid1 = is1 & y_mid
    rodd = row1 & z_odd
    rmid = row1 & z_mid
    top = row1 & (z == 4)
    up2c = remote(cs.at[1], up2, at(z, y_pair, 1, x), cond=y_even)
    side3 = as_int(y % 4 == 3)
    up3c = [remote(cs.at[2], up3.at[i], at(z, y_own, 1, x), cond=odd1 & (side3 == i)) for i in (0, 1)]
    side4 = y // 4
    up4c = [remote(cs.at[3], up4.at[i], at(z, 0, 1, x), cond=mid1 & (side4 == i)) for i in (0, 1)]
    up5c = remote(cs.at[4], up5, at(z_pair, 0, 1, x), cond=row_even)
    side6 = as_int(z % 4 == 3)
    up6c = [remote(cs.at[5], up6.at[i], at(z_own, 0, 1, x), cond=rodd & (side6 == i)) for i in (0, 1)]
    side7 = z // 4
    up7c = [remote(cs.at[6], up7.at[i], at(4, 0, 1, x), cond=rmid & (side7 == i)) for i in (0, 1)]
    to = counter[0]
    dn6 = [
        remote(vb.at[7, i], db.at[6], at(2 + 4 * i, 0, 1, x), cond=top, lands=to)
        for i in (0, 1)
    ]
    to = counter[0]
    dn5 = [
        remote(vb.at[6, i], db.at[5], at(z - 1 + 2 * i, 0, 1, x), cond=rmid, lands=to)
        for i in (0, 1)
    ]
    dn4 = remote(vb.at[5, 0], db.at[4], at(z - 1, 0, 1, x), cond=rodd)
    to = counter[0]
    dn3 = [
        remote(vb.at[4, i], db.at[3], at(z, 2 + 4 * i, 1, x), cond=row1, lands=to)
        for i in (0, 1)
    ]
    to = counter[0]
    dn2 = [
        remote(vb.at[3, i], db.at[2], at(z, y - 1 + 2 * i, 1, x), cond=mid1, lands=to)
        for i in (0, 1)
    ]
    dn1 = remote(vb.at[2, 0], db.at[1], at(z, y - 1, 1, x), cond=odd1)

    def each(side, copies, act):
        for i in (0, 1):
            @when(side == i)
            def _(i=i):
                act(copies[i])

    @when(is0)
    def _():
        core_up.start()

    @when(is1)
    def _():
        core_up_recv.wait_recv()
        cs[1] = up(0, c3l[...], c3[...])

    @when(y_even)
    def _():
        up2c[0].start()

    @when(odd1)
    def _():
        up2c[1].wait_recv()
        cs[2] = up(1, up2[...], cs[1])
        each(side3, up3c, lambda c: c[0].start())

    @when(mid1)
    def _():
        up3c[0][1].wait_recv()
        up3c[1][1].wait_recv()
        cs[3] = up(1, up3[0], up3[1])
        each(side4, up4c, lambda c: c[0].start())

    @when(row1)
    def _():
        up4c[0][1].wait_recv()
        up4c[1][1].wait_recv()
        cs[4] = up(2, up4[0], up4[1])

        @when(z % 2 == 0)
        def _():
            up5c[0].start()

        @when(z_odd)
        def _():
            up5c[1].wait_recv()
            cs[5] = up(1, up5[...], cs[4])
            each(side6, up6c, lambda c: c[0].start())

        @when(z_mid)
        def _():
            up6c[0][1].wait_recv()
            up6c[1][1].wait_recv()
            cs[6] = up(1, up6[0], up6[1])
            each(side7, up7c, lambda c: c[0].start())

        @when(z == 4)
        def _():
            up7c[0][1].wait_recv()
            up7c[1][1].wait_recv()
            wait_factors(0, 1)
            value = nt(jnp.concatenate([up7[0], up7[1]], axis=1), finv[1].reshape(512, 512)).astype(BF)
            vb[7, 0] = value[:, :256]
            vb[7, 1] = value[:, 256:]
            dn6[0][0].start()
            dn6[1][0].start()
            wait_factors(1, 1)
            wait_factors(2, 1)

        @when(z_mid)
        def _():
            dn6[0][1].wait_recv()
            down(1, 6)
            dn5[0][0].start()
            dn5[1][0].start()

        @when(z_odd)
        def _():
            dn5[0][1].wait_recv()
            down(1, 5)
            dn4[0].start()
            db[4] = vb[5, 1]

        @when(z % 2 == 0)
        def _():
            dn4[1].wait_recv()

        @when(z == 0)
        def _():
            for which in range(3):
                wait_factors(which, 1)

        down(2, 4)
        dn3[0][0].start()
        dn3[1][0].start()

    @when(mid1)
    def _():
        dn3[0][1].wait_recv()
        down(1, 3)
        dn2[0][0].start()
        dn2[1][0].start()

    @when(odd1)
    def _():
        dn2[0][1].wait_recv()
        down(1, 2)
        dn1[0].start()
        db[1] = vb[2, 1]

    @when(y_even)
    def _():
        dn1[1].wait_recv()

    @when(is1)
    def _():
        down(0, 1)
        core_down.start()
        db[0] = vb[1, 1]

    @when(is0)
    def _():
        core_down_recv.wait_recv()

    incg[x] = db[0]
    for recv in spread(incg):
        recv.wait_recv()
    for i in (4, 5):
        local[i].wait()
    inc = incg[...].reshape(64, 256)
    d3[x] = (s3[...] - nt(inc, ncou_v[6])).astype(BF)
    for recv in spread(d3):
        recv.wait_recv()
    for n in range(2):
        inc = jnp.concatenate([d3[2 * n], d3[2 * n + 1]], axis=1)
        d2[x, n] = (s2[n] - nt(inc, ncou_v[4 + n])).astype(BF)
    for recv in spread(d2):
        recv.wait_recv()
    for n in range(4):
        half = 2 * (n % 2)
        inc = jnp.concatenate([d2[half, n // 2], d2[half + 1, n // 2]], axis=1)
        d1[x, n] = (s1[n] - nt(inc, ncou_v[n])).astype(BF)
    for recv in spread(d1):
        recv.wait_recv()
    for l in range(8):
        half = 2 * (l % 2)
        inc = jnp.concatenate([d1[half, l // 2], d1[half + 1, l // 2]], axis=1)
        out[l] = lv[l] - nt(inc, lcou_v[l])

    def finish(cond, copy):
        if cond is None:
            copy.wait_send()
        else:
            @when(cond)
            def _():
                copy.wait_send()

    for cond, copy in pending:
        finish(cond, copy)
    for which in range(3):
        for k in (1, 2, 3):
            factor_copy(which, k).wait_send()

        @when(is0)
        def _(which=which):
            factor_copy(which, 0).wait_send()


def body(rs, po, linv, lbas, lcou, ninv, nbas, ncou):
    vm = pl.BlockSpec(memory_space=pltpu.VMEM)
    hbm = pl.BlockSpec(memory_space=pl.ANY)
    dma = pltpu.SemaphoreType.DMA
    scratch = [
        VMEM((3, 64, 1024), BF), VMEM((64, 4096), F32), VMEM((8, 64, 128), F32),
        VMEM((8, 128, 512), BF), VMEM((8, 128, 256), BF), VMEM((8, 128, 256), BF),
        VMEM((7, 128, 512), BF), VMEM((7, 128, 256), BF), VMEM((7, 128, 256), BF),
        VMEM((4, 8, 16, 256), BF), VMEM((3, 8, 16, 256), BF), VMEM((4, 8, 16, 256), BF),
        VMEM((4, 64, 256), BF), VMEM((3, 4, 64, 256), BF), VMEM((4, 64, 256), BF),
        VMEM((2, 64, 256), BF), VMEM((3, 2, 64, 256), BF), VMEM((2, 64, 256), BF),
        VMEM((4, 16, 256), BF), VMEM((3, 16, 256), BF), VMEM((16, 256), BF), VMEM((16, 256), BF),
        VMEM((4, 64, 128), F32), VMEM((2, 64, 128), F32), VMEM((64, 128), F32),
        VMEM((3, 4, 128, 512), BF), VMEM((3, 4, 128, 256), BF), VMEM((3, 4, 128, 256), BF),
        VMEM((3, 16, 512), F32), VMEM((7, 16, 256), BF),
        VMEM((16, 256), BF), VMEM((2, 16, 256), BF), VMEM((2, 16, 256), BF),
        VMEM((16, 256), BF), VMEM((2, 16, 256), BF), VMEM((2, 16, 256), BF),
        VMEM((8, 2, 16, 256), BF), VMEM((7, 16, 256), BF), VMEM((4, 16, 256), BF),
        VMEM((4, 64, 128), BF), VMEM((4, 2, 64, 128), BF), VMEM((4, 4, 64, 128), BF),
        dma((6,)), dma((N_SEMS,)), dma((N_SEMS,)), dma((3, 4)), dma((3, 3, 4)),
    ]
    return pl.pallas_call(
        kernel,
        out_shape=jax.ShapeDtypeStruct((8, 64, 128), F32),
        in_specs=[vm, vm] + [hbm] * 6,
        out_specs=vm,
        scratch_shapes=scratch,
        compiler_params=pltpu.CompilerParams(
            collective_id=0, has_side_effects=True, vmem_limit_bytes=60 << 20
        ),
    )(rs, po.reshape(1, 4096), linv, lbas, lcou, ninv, nbas, ncou)


def solution(mesh):
    placed = (
        P(None, ("leaf", "rhs")),
        P("leaf"),
        P("leaf", "rhs", None),
        P("leaf", "rhs", None),
        P("leaf", "rhs", None),
        P("leaf", "rhs", None),
        P("leaf", "rhs", None),
        P("leaf", "rhs", None),
    )
    return jax.shard_map(
        body, mesh=mesh, in_specs=placed, out_specs=P("leaf", None, "rhs"), check_vma=False
    )
```

time: 477 us -> 116 us (0.24)
  the two profiles are of different devices: /device:TPU:256 before, /device:TPU:4 now
where the time goes in v1:
time: 116 us
  Pallas kernels  114 us (98%)
  local copies, waits for them, and re-layouts  1.67 us (1%)
    pallas_call x1, Pallas kernels, body(): pl.pallas_call(kernel, out_shape=jax.ShapeDtypeStruct((8, 64, 128), F32),...  114 us

profile of v1, /device:TPU:4, one launch (start us, length us, event | category | flops | bytes accessed | tf_op | source)
XLA Modules:
  0.0 115.6 jit_solution(14263054421432505439)
XLA Ops:
  0.0 113.9 %shard_map.82 = f32[8,64,128]{2,1,0:T(8,128)} custom-call(bf16[64,1024]{1,0:T(8,128)(2,1)} %rs.1, s32[1,4096]{1,0:T(1,128)} %bitcast.1, bf16[8,128,512]{2,1,0:T(8,128)(2,1)} %linv.1, bf16[8,128,256]{2,1,0:T(8,128)(2,1)} %lbas.1, bf16[8,128,256]{2,1,0:T(8,128)(2,1)} %lcou.1, bf16[8,128,512]{2,1,0:T(8,128)(2,1)} %ninv.1, bf16[8,128,256]{2,1,0:T(8,128)(2,1)} %nbas.1, ...), custom_call_target="tpu_custom_call" | custom-call | tf_op jit(solution)/shard_map/pallas_call | solution.py:533
  113.9 1.7 %copy.10 = f32[8,64,128]{2,1,0:T(8,128)} copy(f32[8,64,128]{2,1,0:T(8,128)} %shard_map.82) | data formatting | bytes 524288

commit v2 on v0

v2 whole, which is shorter than its diff:
```python
import jax
import jax.numpy as jnp
from jax import lax
from jax.experimental import pallas as pl
from jax.experimental.pallas import tpu as pltpu
from jax.sharding import PartitionSpec as P

MESH = pl.DeviceIdType.MESH
BF = jnp.bfloat16
F32 = jnp.float32
VMEM = pltpu.VMEM
HOME = 1
HIGH = 2
N_SEMS = 128
ALONG_X = (1, 3, 2)
WHEN = {0: (), 1: ("fi", "fb", "n1i", "n1b"), 2: (), 3: (), 4: ("n2i", "n2b", "pi", "pb"), 5: (), 6: ("fc",), 7: ("c1", "pc")}


def nt(a, b):
    return lax.dot_general(a, b, (((1,), (1,)), ((), ())), preferred_element_type=F32)


def nn(a, b):
    return lax.dot_general(a, b, (((1,), (0,)), ((), ())), preferred_element_type=F32)


def xor(a, k):
    total = 0
    for bit in (1, 2):
        digit = (a // bit) % 2
        total = total + bit * ((1 - digit) if k & bit else digit)
    return total


def as_int(cond):
    return jnp.where(cond, 1, 0)


def kernel(
    rs, po, linv, lbas, lcou, ninv, nbas, ncou, out,
    tg, acc, lv, linv_v, lbas_v, lcou_v, rsb, rsr,
    n1i, n1b, n1c, n2i, n2b, c2h, c3h,
    s1, s2b, s3b, s2h, s3h, cb1, u2x, cb2, u3x,
    finv, fbas, fcou, fs1, fsv, fsz, cs, u1, u2, u34, u5, u67,
    sh2, sh5, sb2, sb5, id2, id5, vy, vz, vcore, inc3, i0,
    lsem, ssem, rsem, fss, frs,
):
    leaf = lax.axis_index("leaf")
    x = lax.axis_index("rhs")
    core = leaf % 2
    y = (leaf // 2) % 8
    z = leaf // 16

    def at(z_, y_, c_, x_):
        return ((z_ * 8 + y_) * 2 + c_, x_)

    counter = [0]
    pending = []

    def remote(src, dst, target, my_dst=None, cond=None, lands=None):
        i = counter[0]
        counter[0] += 1
        j = i if lands is None else lands
        made = [
            pltpu.make_async_remote_copy(
                src_ref=src, dst_ref=here, send_sem=ssem.at[i], recv_sem=rsem.at[j],
                device_id=target, device_id_type=MESH,
            )
            for here in (dst, dst if my_dst is None else my_dst)
        ]
        pending.append((cond, made[0]))
        return made

    def begin(copy, cond=None):
        if cond is None:
            copy.start()
        else:
            @pl.when(cond)
            def _():
                copy.start()

    local_count = [0]

    def local(src, dst):
        i = local_count[0]
        local_count[0] += 1
        return pltpu.make_async_copy(src, dst, lsem.at[i])

    xs = [xor(x, k) for k in range(4)]
    is0 = core == 0
    is1 = core == 1
    y_odd = y % 2 == 1
    z_odd = z % 2 == 1
    y_pair = y + 1 - 2 * (y % 2)
    z_pair = z + 1 - 2 * (z % 2)
    home = x == HOME
    plane = is1 & home
    high = is1 & (x == HIGH)
    spine = high & (y == 0)
    top = spine & (z == 4)
    low = x < 2

    own_linv, own_lbas, own_lcou = (
        local(linv, linv_v), local(lbas, lbas_v), local(lcou, lcou_v)
    )
    own_n1 = [local(a.at[x], b.at[x]) for a, b in ((ninv, n1i), (nbas, n1b), (ncou, n1c))]
    for copy in [own_linv, own_lbas, own_lcou] + own_n1:
        copy.start()

    def entry(at_x):
        return 4 + as_int(at_x == 1) * 2 + as_int(at_x == 2)

    has_n2 = x != 3
    own_entry = jnp.where(has_n2, entry(x), 4)
    own_n2 = [local(a.at[own_entry], b.at[x]) for a, b in ((ninv, n2i), (nbas, n2b))]
    for copy in own_n2:
        copy.start()

    barrier = pltpu.get_barrier_semaphore()

    def greet(*target):
        pl.semaphore_signal(barrier, inc=1, device_id=at(*target), device_id_type=MESH)

    def greet_if(cond, *targets):
        @pl.when(cond)
        def _():
            for target in targets:
                greet(*target)

    for k in ALONG_X:
        greet(z, y, core, xs[k])
    greet(z, y, 1 - core, x)
    odds = (1, 3, 5, 7)
    y_even = y % 2 == 0
    z_even = z % 2 == 0
    greet_if(plane & y_odd, *[(z, y, 0, r) for r in (2, 3)])
    greet_if(plane & y_even, *[(z, y + 1, 0, r) for r in (0, 1)])
    greet_if(plane, (z, y + as_int(y_even), 1, HIGH), (z, 0, 1, HIGH))
    greet_if(high & y_odd, *[(z, y, 0, r) for r in range(4)])
    greet_if(high & y_odd, (z, y, 1, HOME), (z, y - 1, 1, HOME))
    greet_if(high & y_even & (y > 0), *[(z, y, 0, r) for r in range(4)])
    greet_if(spine, *[(z, t, 1, HIGH) for t in range(1, 8)])
    greet_if(spine, (z_pair, 0, 1, HIGH))
    greet_if(spine & (z > 0), *[(z, 0, 0, r) for r in range(4)])
    greet_if(spine & z_even, *[(z + 1, 0, 0, r) for r in (0, 1)])
    greet_if(spine & (z != 4), (4, 0, 1, HIGH))
    greet_if(top, *[(t, 0, 1, HIGH) for t in (1, 2, 3, 5, 6, 7)])
    mover = jnp.where(y > 0, 1 + as_int(y_odd), as_int(z > 0) + as_int(z_odd & low))
    expect = (
        4
        + as_int(is0) * mover
        + as_int(plane)
        + as_int(high & y_odd) * 3
        + as_int(high & y_even & (y > 0))
        + as_int(spine) * (9 + as_int(z_odd) + as_int(z % 4 == 2))
        + as_int(top) * 7
    )
    pl.semaphore_wait(barrier, expect)

    gather = {k: remote(rs, tg.at[k - 1], at(z, y, core, xs[k])) for k in ALONG_X}
    gather[1][0].start()
    gather[3][0].start()

    def along_x(src, dst, k, cond=None):
        return remote(src, dst.at[x], at(z, y, core, xs[k]), my_dst=dst.at[xs[k]], cond=cond)

    move_n1 = [along_x(a.at[xs[k]], b, k) for a, b in ((ninv, n1i), (nbas, n1b)) for k in ALONG_X]
    move_c1 = [along_x(ncou.at[xs[k]], n1c, k) for k in ALONG_X]
    goes_n2 = {k: xs[k] != 3 for k in ALONG_X}
    move_n2 = [
        along_x(a.at[jnp.where(goes_n2[k], entry(xs[k]), 4)], b, k, cond=goes_n2[k])
        for a, b in ((ninv, n2i), (nbas, n2b))
        for k in ALONG_X
    ]

    first_row = is0 & (y == 0)
    slot = jnp.where(
        is1,
        0,
        jnp.where(
            y > 0,
            jnp.where(y_odd, 1, jnp.where(y == 2, 2, jnp.where(y == 6, 3, 4))),
            jnp.where(z_odd, 1, jnp.where(z == 2, 5, jnp.where(z == 6, 6, 7))),
        ),
    )
    halved_y = is0 & y_odd
    halved_z = first_row & z_odd
    slot_c = jnp.where(halved_y, 8, jnp.where(halved_z, 9, slot))
    to_y_c = y - as_int(halved_y & low)
    to_z_c = z - as_int(halved_z & low)
    stays = plane
    to_x = jnp.where(is1, HOME, HIGH)
    to_x_c = jnp.where(halved_y, HOME, to_x)
    has_inv = jnp.logical_not(first_row & (z == 0)) & jnp.logical_not(stays)
    has_rest = has_inv & jnp.logical_not(first_row & (z == 4))
    factors = ((ninv.at[7], finv), (nbas.at[7], fbas), (ncou.at[7], fcou))

    def factor_copy(which):
        src, dst = factors[which]
        place = slot_c if which == 2 else slot
        target = at(to_z_c, to_y_c, 1, to_x_c) if which == 2 else at(z, y, 1, to_x)
        return pltpu.make_async_remote_copy(
            src_ref=src, dst_ref=dst.at[place, x], send_sem=fss.at[which],
            recv_sem=frs.at[which, place, x], device_id=target, device_id_type=MESH,
        )

    def factor_own(which):
        src, dst = factors[which]
        return pltpu.make_async_copy(src, dst.at[0, HOME], fss.at[which])

    def send_factors(which):
        begin(factor_copy(which), has_inv if which == 0 else has_rest)
        begin(factor_own(which), stays)

    def wait_factor(which, place, r):
        src, dst = factors[which]
        pltpu.make_async_remote_copy(
            src_ref=src, dst_ref=dst.at[place, r], send_sem=fss.at[which],
            recv_sem=frs.at[which, place, r], device_id=at(z, y, 0, x), device_id_type=MESH,
        ).wait_recv()

    def wait_factors(which, place):
        for r in range(4):
            if place == 0 and r == HOME:
                factor_own(which).wait()
            else:
                wait_factor(which, place, r)

    def start_all(moves, conds=None):
        for n, (send, _) in enumerate(moves):
            begin(send, conds[n] if conds else None)

    n2_conds = [goes_n2[k] for k in ALONG_X]
    items = {
        "n1i": lambda: start_all(move_n1[:3]),
        "n1b": lambda: start_all(move_n1[3:]),
        "n2i": lambda: start_all(move_n2[:3], n2_conds),
        "n2b": lambda: start_all(move_n2[3:], n2_conds),
        "fi": lambda: send_factors(0),
        "fb": lambda: send_factors(1),
        "fc": lambda: send_factors(2),
        "c1": lambda: start_all(move_c1),
        "pi": lambda: pass_on(0),
        "pb": lambda: pass_on(1),
        "pc": lambda: pass_on(2),
    }

    def point(n):
        for item in WHEN[n]:
            items[item]()

    passing = [(2, high & (y == 2), (z, 0)), (3, high & (y == 6), (z, 0)), (4, high & (y == 4), (z, 0))]
    passing += [(5, spine & (z == 2), (4, 0)), (6, spine & (z == 6), (4, 0))]
    passed = {
        (which, place): remote(
            factors[which][1].at[place], factors[which][1].at[place], at(*to, 1, HIGH), cond=cond
        )
        for place, cond, to in passing
        for which in range(3)
    }

    def pass_on(which):
        for place, cond, _ in passing:
            @pl.when(cond)
            def _(place=place):
                wait_factors(which, place)
                passed[which, place][0].start()

    wide = 512

    def permute(block, source, first):
        base = source * 1024

        def part(j, carry):
            cols = pl.ds(pl.multiple_of(j * wide, wide), wide)
            rows = lax.broadcasted_iota(jnp.int32, (1024, wide), 0) + base
            hot = jnp.where(rows == po[:, cols], 1.0, 0.0).astype(BF)
            term = nn(block, hot)
            acc[:, cols] = term if first else acc[:, cols] + term
            return carry

        lax.fori_loop(0, 4096 // wide, part, 0)

    point(0)
    permute(rs[...], x, True)
    gather[2][0].start()
    point(1)
    gather[1][1].wait_recv()
    permute(tg[0], xs[1], False)
    point(2)
    gather[3][1].wait_recv()
    permute(tg[2], xs[3], False)
    point(3)
    gather[2][1].wait_recv()
    permute(tg[1], xs[2], False)

    own_linv.wait()
    own_lbas.wait()
    scatter = {k: remote(rsb.at[xs[k]], rsr.at[k - 1], at(z, y, core, xs[k])) for k in ALONG_X}
    for k in (2, 1, 3, 0):
        for j in range(2):
            l = 2 * xs[k] + j
            cols = pl.ds(pl.multiple_of(l * 512, 512), 512)
            value = nt(acc[:, cols].astype(BF), linv_v[l])
            lv[l] = value
            rsb[xs[k], j] = nn(value.astype(BF), lbas_v[l]).astype(BF)
        if k:
            scatter[k][0].start()
    point(4)
    for k in ALONG_X:
        scatter[k][1].wait_recv()

    def summed(j):
        total = rsb[x, j].astype(F32)
        for k in range(3):
            total = total + rsr[k, j].astype(F32)
        return total.astype(BF)

    def solve(left, right, inverse):
        return nt(jnp.concatenate([left, right], axis=1), inverse.reshape(512, 512))

    def squeeze(solved, basis):
        return nn(solved.astype(BF), basis.reshape(512, 256)).astype(BF)

    point(5)
    for _, recv in move_n1:
        recv.wait_recv()
    own_n1[0].wait()
    own_n1[1].wait()
    solved = solve(summed(0), summed(1), n1i[...])
    s1[...] = solved
    cb1[...] = squeeze(solved, n1b[...])

    x_odd = x % 2 == 1
    x_even = x % 2 == 0
    up_l1 = remote(cb1, u2x, at(z, y, core, xs[1]), cond=x_odd)
    to_home = counter[0]
    up_l2 = [
        remote(cb2, u3x.at[i], at(z, y, core, HOME), cond=x == 2 * i) for i in (0, 1)
    ]
    share_s2 = remote(s2b.at[1], s2h, at(z, y, core, xs[1]), cond=x_even)
    landing = counter[0]
    share_s3 = {
        t: remote(s3b.at[t // 2], s3h, at(z, y, core, t), cond=home, lands=landing) for t in (0, 2, 3)
    }
    begin(up_l1[0], x_odd)
    point(6)

    own_n2[0].wait()
    own_n2[1].wait()

    @pl.when(has_n2)
    def _():
        for _, recv in move_n2:
            recv.wait_recv()

    @pl.when(x_even)
    def _():
        up_l1[1].wait_recv()
        solved = solve(cb1[...], u2x[...], n2i[...])
        cb2[...] = squeeze(solved, n2b[...])
        for i in (0, 1):
            begin(up_l2[i][0], x == 2 * i)
        rounded = solved.astype(BF)
        s2b[1] = rounded[:, 256:]
        s2h[...] = rounded[:, :256]
        share_s2[0].start()

    @pl.when(home)
    def _():
        for i in (0, 1):
            up_l2[i][1].wait_recv()
        solved = solve(u3x[0], u3x[1], n2i[...])
        cb2[...] = squeeze(solved, n2b[...])
        rounded = solved.astype(BF)
        s3b[0] = rounded[:, :256]
        s3b[1] = rounded[:, 256:]

    cross_up = remote(cb2, u1, at(z, y, 1, x), cond=is0 & home)
    begin(cross_up[0], is0 & home)
    for t in (0, 2, 3):
        begin(share_s3[t][0], home)

    @pl.when(home)
    def _():
        s3h[...] = s3b[HOME // 2]

    high_odd = high & y_odd
    spine_odd = spine & z_odd
    spine_even = spine & z_even
    y_own = y + as_int(y_even)
    up2 = [
        remote(cs.at[0], u2.at[i], at(z, y_own, 1, HIGH), cond=plane & (y % 2 == i)) for i in (0, 1)
    ]
    landing = counter[0]
    share2 = [
        remote(sb2.at[i], sh2, at(z, y - 1 + i, 1, HOME), cond=high_odd, lands=landing) for i in (0, 1)
    ]
    up34 = [
        remote(cs.at[1], u34.at[m], at(z, 0, 1, x), cond=high & (y == 2 * m + 1)) for m in range(4)
    ]
    up5 = remote(cs.at[2], u5, at(z_pair, 0, 1, x), cond=spine_even)
    share5 = remote(sb5, sh5, at(z_pair, 0, 1, x), cond=spine_odd)
    up67 = [
        remote(cs.at[3], u67.at[m], at(4, 0, 1, x), cond=spine & (z == 2 * m + 1)) for m in range(4)
    ]
    landing = counter[0]
    down_z = {
        t: remote(vz.at[t // 2], id5, at(t, 0, 1, x), cond=top, lands=landing)
        for t in (0, 1, 2, 3, 5, 6, 7)
    }
    landing = counter[0]
    down_y = {
        t: remote(vy.at[t // 2], id2, at(z, t, 1, HOME), cond=spine, lands=landing) for t in range(8)
    }
    cross_down = remote(vcore, inc3, at(z, y, 0, x), cond=plane)

    @pl.when(plane)
    def _():
        wait_factors(0, 0)
        wait_factors(1, 0)
        cross_up[1].wait_recv()
        solved = solve(u1[...], cb2[...], finv[0])
        cs[0] = squeeze(solved, fbas[0])
        for i in (0, 1):
            begin(up2[i][0], y % 2 == i)
        fs1[...] = solved

    @pl.when(high_odd)
    def _():
        wait_factors(0, 1)
        wait_factors(1, 1)
        for i in (0, 1):
            up2[i][1].wait_recv()
        solved = solve(u2[0], u2[1], finv[1])
        cs[1] = squeeze(solved, fbas[1])
        for m in range(4):
            begin(up34[m][0], y == 2 * m + 1)
        rounded = solved.astype(BF)
        for i in (0, 1):
            sb2[i] = rounded[:, 256 * i : 256 * i + 256]
            share2[i][0].start()

    def pair_up(arrived, buffer, first, store):
        squeezed = []
        for i in (0, 1):
            arrived[2 * i][1].wait_recv()
            arrived[2 * i + 1][1].wait_recv()
            solved = solve(buffer[2 * i], buffer[2 * i + 1], finv[first + i])
            store[i] = solved
            squeezed.append(squeeze(solved, fbas[first + i]))
        return solve(squeezed[0], squeezed[1], finv[first + 2])

    def pair_down(value, first, buffer, copies, own, store):
        value = value.astype(BF)
        for i in (0, 1):
            inc = value[:, 256 * i : 256 * i + 256]
            child = (store[i] - nt(inc, fcou[first + i].reshape(512, 256))).astype(BF)
            for j in (0, 1):
                buffer[2 * i + j] = child[:, 256 * j : 256 * j + 256]
            for t in range(4 * i, 4 * i + 4):
                if t != own:
                    copies[t][0].start()

    @pl.when(top)
    def _():
        for place in (5, 6):
            passed[0, place][1].wait_recv()
            passed[1, place][1].wait_recv()
        wait_factors(0, 7)

    @pl.when(spine)
    def _():
        for place in (2, 3, 4):
            passed[0, place][1].wait_recv()
            passed[1, place][1].wait_recv()
        solved = pair_up(up34, u34, 2, fsv)
        cs[2] = squeeze(solved, fbas[4])
        fsv[2] = solved
        begin(up5[0], z % 2 == 0)

        @pl.when(z_odd)
        def _():
            wait_factors(0, 1)
            wait_factors(1, 1)
            up5[1].wait_recv()
            solved = solve(u5[...], cs[2], finv[1])
            cs[3] = squeeze(solved, fbas[1])
            for m in range(4):
                begin(up67[m][0], z == 2 * m + 1)
            rounded = solved.astype(BF)
            sb5[...] = rounded[:, :256]
            sh5[...] = rounded[:, 256:]
            share5[0].start()

    point(7)
    own_c3 = local(ncou.at[6], c3h.at[x % 2])
    own_c3.start()
    send_c3 = remote(ncou.at[6], c3h.at[x % 2], at(z, y, core, xs[1]), my_dst=c3h.at[xs[1] % 2])
    send_c3[0].start()
    c2_sem = counter[0]
    counter[0] += 4
    c2_away = []
    for m in (0, 1):
        target = 2 * m + x // 2
        copy = pltpu.make_async_remote_copy(
            src_ref=ncou.at[4 + m], dst_ref=c2h.at[x % 2], send_sem=ssem.at[c2_sem + m],
            recv_sem=rsem.at[c2_sem + x % 2], device_id=at(z, y, core, target), device_id_type=MESH,
        )
        away = target != x
        pending.append((away, copy))
        c2_away.append((copy, away))
        begin(copy, away)
    own_c2 = local(ncou.at[4 + x // 2], c2h.at[x % 2])
    own_c2_here = (x == 0) | (x == 3)
    begin(own_c2, own_c2_here)

    @pl.when(top)
    def _():
        solved = pair_up(up67, u67, 5, fsz)
        passed[2, 5][1].wait_recv()
        passed[2, 6][1].wait_recv()
        pair_down(solved, 5, vz, down_z, 4, fsz)
        id5[...] = vz[2]

    @pl.when(spine)
    def _():
        for place in (2, 3, 4):
            passed[2, place][1].wait_recv()
        half = 2 * (z % 2)
        for j in (0, 1):
            wait_factor(2, 9, half + j)

        @pl.when(z != 4)
        def _():
            down_z[0][1].wait_recv()

        @pl.when(z % 2 == 0)
        def _():
            share5[1].wait_recv()

        rows = fcou[9, pl.ds(half, 2)].reshape(256, 256)
        inc = (sh5[...].astype(F32) - nt(id5[...], rows)).astype(BF)
        value = fsv[2] - nt(inc, fcou[4].reshape(512, 256))
        pair_down(value, 2, vy, down_y, -1, fsv)

    @pl.when(plane)
    def _():
        wait_factors(2, 0)
        half = 2 * (y % 2)
        for j in (0, 1):
            wait_factor(2, 8, half + j)

        down_y[0][1].wait_recv()
        share2[0][1].wait_recv()

        rows = fcou[8, pl.ds(half, 2)].reshape(256, 256)
        inc = (sh2[...].astype(F32) - nt(id2[...], rows)).astype(BF)
        value = (fs1[...] - nt(inc, fcou[0].reshape(512, 256))).astype(BF)
        vcore[...] = value[:, :256]
        cross_down[0].start()
        inc3[...] = value[:, 256:]

    @pl.when(is0 & home)
    def _():
        cross_down[1].wait_recv()

    landing = counter[0]
    inc_in = {
        t: remote(inc3, inc3, at(z, y, core, t), cond=home, lands=landing) for t in (0, 2, 3)
    }
    for t in (0, 2, 3):
        begin(inc_in[t][0], home)

    for _, recv in move_c1:
        recv.wait_recv()
    own_n1[2].wait()
    own_c3.wait()
    send_c3[1].wait_recv()
    from_x = 2 * (x % 2)
    for j in (0, 1):
        @pl.when(from_x + j != x)
        def _(j=j):
            pltpu.make_async_remote_copy(
                src_ref=ncou.at[4], dst_ref=c2h.at[j], send_sem=ssem.at[c2_sem],
                recv_sem=rsem.at[c2_sem + j], device_id=at(z, y, core, xs[1]), device_id_type=MESH,
            ).wait_recv()

    @pl.when(own_c2_here)
    def _():
        own_c2.wait()

    @pl.when(x_odd)
    def _():
        share_s2[1].wait_recv()

    @pl.when(jnp.logical_not(home))
    def _():
        share_s3[0][1].wait_recv()
        inc_in[0][1].wait_recv()

    value = (s3h[...].astype(F32) - nt(inc3[...], c3h[...].reshape(256, 256))).astype(BF)
    value = (s2h[...].astype(F32) - nt(value, c2h[...].reshape(256, 256))).astype(BF)
    value = (s1[...] - nt(value, n1c[...].reshape(512, 256))).astype(BF)
    i0[x, 0] = value[:, :256]
    i0[x, 1] = value[:, 256:]
    spread = {
        k: remote(i0.at[x], i0.at[x], at(z, y, core, xs[k]), my_dst=i0.at[xs[k]]) for k in ALONG_X
    }
    for k in ALONG_X:
        spread[k][0].start()
    own_lcou.wait()
    for k in (0, 1, 3, 2):
        if k:
            spread[k][1].wait_recv()
        for j in range(2):
            l = 2 * xs[k] + j
            out[l] = lv[l] - nt(i0[xs[k], j], lcou_v[l])

    def left(copy, cond):
        if cond is None:
            copy.wait_send()
        else:
            @pl.when(cond)
            def _():
                copy.wait_send()

    for cond, copy in pending:
        left(copy, cond)
    left(factor_copy(0), has_inv)
    left(factor_copy(1), has_rest)
    left(factor_copy(2), has_rest)


def body(rs, po, linv, lbas, lcou, ninv, nbas, ncou):
    vm = pl.BlockSpec(memory_space=pltpu.VMEM)
    hbm = pl.BlockSpec(memory_space=pl.ANY)
    dma = pltpu.SemaphoreType.DMA
    part = VMEM((64, 256), BF)
    scratch = [
        VMEM((3, 64, 1024), BF), VMEM((64, 4096), F32), VMEM((8, 64, 128), F32),
        VMEM((8, 128, 512), BF), VMEM((8, 128, 256), BF), VMEM((8, 128, 256), BF),
        VMEM((4, 2, 64, 256), BF), VMEM((3, 2, 64, 256), BF),
        VMEM((4, 128, 512), BF), VMEM((4, 128, 256), BF), VMEM((4, 128, 256), BF),
        VMEM((4, 128, 512), BF), VMEM((4, 128, 256), BF),
        VMEM((2, 128, 256), BF), VMEM((2, 128, 256), BF),
        VMEM((64, 512), F32), VMEM((2, 64, 256), BF), VMEM((2, 64, 256), BF), part, part,
        part, part, part, VMEM((2, 64, 256), BF),
        VMEM((8, 4, 128, 512), BF), VMEM((8, 4, 128, 256), BF), VMEM((10, 4, 128, 256), BF),
        VMEM((64, 512), F32), VMEM((3, 64, 512), F32), VMEM((2, 64, 512), F32), VMEM((4, 64, 256), BF),
        part, VMEM((2, 64, 256), BF), VMEM((4, 64, 256), BF), part, VMEM((4, 64, 256), BF),
        part, part, VMEM((2, 64, 256), BF), part, part, part, VMEM((4, 64, 256), BF), VMEM((4, 64, 256), BF),
        part, part, VMEM((4, 2, 64, 256), BF),
        dma((12,)), dma((N_SEMS,)), dma((N_SEMS,)), dma((3,)), dma((3, 10, 4)),
    ]
    return pl.pallas_call(
        kernel,
        out_shape=jax.ShapeDtypeStruct((8, 64, 128), F32),
        in_specs=[vm, vm] + [hbm] * 6,
        out_specs=vm,
        scratch_shapes=scratch,
        compiler_params=pltpu.CompilerParams(
            collective_id=0, has_side_effects=True, vmem_limit_bytes=60 << 20
        ),
    )(rs, po.reshape(1, 4096), linv, lbas, lcou, ninv, nbas, ncou)


def solution(mesh):
    placed = (
        P(None, ("leaf", "rhs")),
        P("leaf"),
        P("leaf", "rhs", None),
        P("leaf", "rhs", None),
        P("leaf", "rhs", None),
        P("leaf", "rhs", None),
        P("leaf", "rhs", None),
        P("leaf", "rhs", None),
    )
    return jax.shard_map(
        body, mesh=mesh, in_specs=placed, out_specs=P("leaf", None, "rhs"), check_vma=False
    )
```

time: 477 us -> 91.4 us (0.19)
  the two profiles are of different devices: /device:TPU:256 before, /device:TPU:32 now
where the time goes in v2:
time: 91.4 us; the launch traced here: 91.3 us
  Pallas kernels  89.6 us (98%)
  local copies, waits for them, and re-layouts  1.67 us (2%)
    pallas_call x1, Pallas kernels, body(): pl.pallas_call(kernel, out_shape=jax.ShapeDtypeStruct((8, 64, 128), F32),...  89.6 us

profile of v2, /device:TPU:32, one launch (start us, length us, event | category | flops | bytes accessed | tf_op | source)
XLA Modules:
  0.0 91.3 jit_solution(15653904781486920431)
XLA Ops:
  0.0 89.6 %shard_map.82 = f32[8,64,128]{2,1,0:T(8,128)} custom-call(bf16[64,1024]{1,0:T(8,128)(2,1)} %rs.1, s32[1,4096]{1,0:T(1,128)} %bitcast.1, bf16[8,128,512]{2,1,0:T(8,128)(2,1)} %linv.1, bf16[8,128,256]{2,1,0:T(8,128)(2,1)} %lbas.1, bf16[8,128,256]{2,1,0:T(8,128)(2,1)} %lcou.1, bf16[8,128,512]{2,1,0:T(8,128)(2,1)} %ninv.1, bf16[8,128,256]{2,1,0:T(8,128)(2,1)} %nbas.1, ...), custom_call_target="tpu_custom_call" | custom-call | tf_op jit(solution)/shard_map/pallas_call | solution.py:656
  89.6 1.7 %copy.10 = f32[8,64,128]{2,1,0:T(8,128)} copy(f32[8,64,128]{2,1,0:T(8,128)} %shard_map.82) | data formatting | bytes 524288

commit v3 on v2

--- a/solution.py
+++ b/solution.py
@@ -13,7 +13,7 @@
 HIGH = 2
 N_SEMS = 128
 ALONG_X = (1, 3, 2)
-WHEN = {0: (), 1: ("fi", "fb", "n1i", "n1b"), 2: (), 3: (), 4: ("n2i", "n2b", "pi", "pb"), 5: (), 6: ("fc",), 7: ("c1", "pc")}
+WHEN = {0: (), 1: ("fi", "fb", "n1i", "n1b"), 2: (), 3: (), 4: (), 5: ("n2",), 6: ("pi", "pb", "n3"), 7: ("fc", "c1", "pc")}
 
 
 def nt(a, b):
@@ -38,7 +38,7 @@
 
 def kernel(
     rs, po, linv, lbas, lcou, ninv, nbas, ncou, out,
-    tg, acc, lv, linv_v, lbas_v, lcou_v, rsb, rsr,
+    tg, spots, acc, lv, linv_v, lbas_v, lcou_v, rsb, rsr,
     n1i, n1b, n1c, n2i, n2b, c2h, c3h,
     s1, s2b, s3b, s2h, s3h, cb1, u2x, cb2, u3x,
     finv, fbas, fcou, fs1, fsv, fsz, cs, u1, u2, u34, u5, u67,
@@ -160,6 +160,7 @@
     gather = {k: remote(rs, tg.at[k - 1], at(z, y, core, xs[k])) for k in ALONG_X}
     gather[1][0].start()
     gather[3][0].start()
+    gather[2][0].start()
 
     def along_x(src, dst, k, cond=None):
         return remote(src, dst.at[x], at(z, y, core, xs[k]), my_dst=dst.at[xs[k]], cond=cond)
@@ -230,12 +231,13 @@
         for n, (send, _) in enumerate(moves):
             begin(send, conds[n] if conds else None)
 
-    n2_conds = [goes_n2[k] for k in ALONG_X]
+    level2_conds = [xs[k] % 2 == 0 for k in ALONG_X] * 2
+    level3_conds = [xs[k] == HOME for k in ALONG_X] * 2
     items = {
         "n1i": lambda: start_all(move_n1[:3]),
         "n1b": lambda: start_all(move_n1[3:]),
-        "n2i": lambda: start_all(move_n2[:3], n2_conds),
-        "n2b": lambda: start_all(move_n2[3:], n2_conds),
+        "n2": lambda: start_all(move_n2, level2_conds),
+        "n3": lambda: start_all(move_n2, level3_conds),
         "fi": lambda: send_factors(0),
         "fb": lambda: send_factors(1),
         "fc": lambda: send_factors(2),
@@ -266,24 +268,25 @@
                 wait_factors(which, place)
                 passed[which, place][0].start()
 
-    wide = 512
+    def find_spots(j, carry):
+        cols = pl.ds(pl.multiple_of(j * 512, 512), 512)
+        rows = lax.broadcasted_iota(jnp.int32, (256, 512), 0)
+        spots[:, cols] = jnp.where(rows == po[:, cols] % 256, 1.0, 0.0).astype(BF)
+        return carry
+
+    lax.fori_loop(0, 8, find_spots, 0)
 
     def permute(block, source, first):
-        base = source * 1024
-
-        def part(j, carry):
-            cols = pl.ds(pl.multiple_of(j * wide, wide), wide)
-            rows = lax.broadcasted_iota(jnp.int32, (1024, wide), 0) + base
-            hot = jnp.where(rows == po[:, cols], 1.0, 0.0).astype(BF)
-            term = nn(block, hot)
-            acc[:, cols] = term if first else acc[:, cols] + term
-            return carry
-
-        lax.fori_loop(0, 4096 // wide, part, 0)
+        group = po[...] // 256 - source * 4
+        stacked = jnp.concatenate([block[:, 256 * g : 256 * g + 256] for g in range(4)], axis=0)
+        candidates = nn(stacked, spots[...])
+        value = jnp.zeros((64, 4096), F32) if first else acc[...]
+        for g in range(4):
+            value = jnp.where(group == g, candidates[64 * g : 64 * g + 64], value)
+        acc[...] = value
 
     point(0)
     permute(rs[...], x, True)
-    gather[2][0].start()
     point(1)
     gather[1][1].wait_recv()
     permute(tg[0], xs[1], False)
@@ -638,7 +641,7 @@
     dma = pltpu.SemaphoreType.DMA
     part = VMEM((64, 256), BF)
     scratch = [
-        VMEM((3, 64, 1024), BF), VMEM((64, 4096), F32), VMEM((8, 64, 128), F32),
+        VMEM((3, 64, 1024), BF), VMEM((256, 4096), BF), VMEM((64, 4096), F32), VMEM((8, 64, 128), F32),
         VMEM((8, 128, 512), BF), VMEM((8, 128, 256), BF), VMEM((8, 128, 256), BF),
         VMEM((4, 2, 64, 256), BF), VMEM((3, 2, 64, 256), BF),
         VMEM((4, 128, 512), BF), VMEM((4, 128, 256), BF), VMEM((4, 128, 256), BF),

time: 91.4 us -> 90 us (0.985)
  Pallas kernels: 89.6 us -> 88.2 us
    pallas_call x1, Pallas kernels: 89.6 us -> 88.2 us  [body(): pl.pallas_call(kernel, out_shape=jax.ShapeDtypeStruct((8, 64, 128), F32),...]
where the time goes in v3:
time: 90 us; the launch traced here: 89.8 us
  Pallas kernels  88.2 us (98%)
  local copies, waits for them, and re-layouts  1.67 us (2%)
    pallas_call x1, Pallas kernels, body(): pl.pallas_call(kernel, out_shape=jax.ShapeDtypeStruct((8, 64, 128), F32),...  88.2 us

profile of v3, /device:TPU:32, one launch (start us, length us, event | category | flops | bytes accessed | tf_op | source)
XLA Modules:
  0.0 89.8 jit_solution(3613650145472121113)
XLA Ops:
  0.0 88.2 %shard_map.82 = f32[8,64,128]{2,1,0:T(8,128)} custom-call(bf16[64,1024]{1,0:T(8,128)(2,1)} %rs.1, s32[1,4096]{1,0:T(1,128)} %bitcast.1, bf16[8,128,512]{2,1,0:T(8,128)(2,1)} %linv.1, bf16[8,128,256]{2,1,0:T(8,128)(2,1)} %lbas.1, bf16[8,128,256]{2,1,0:T(8,128)(2,1)} %lcou.1, bf16[8,128,512]{2,1,0:T(8,128)(2,1)} %ninv.1, bf16[8,128,256]{2,1,0:T(8,128)(2,1)} %nbas.1, ...), custom_call_target="tpu_custom_call" | custom-call | tf_op jit(solution)/shard_map/pallas_call | solution.py:659
  88.2 1.7 %copy.10 = f32[8,64,128]{2,1,0:T(8,128)} copy(f32[8,64,128]{2,1,0:T(8,128)} %shard_map.82) | data formatting | bytes 524288
